TPU v7x, 256 devices: a whole 4x4x8 slice. The times are simulated.
256 devices in a mesh: sector: 16 (over y, x), bin: 16 (over z, core).
Axes of the slice: x: 4, y: 4, z: 8, core: 2. Of those that a mesh axis runs over, the one named last changes fastest.
Arguments:
- sph_state: float32 [7, 262144], P(None, ('sector', 'bin')), as said below
- sph_dest: int32 [262144, 1], P(('sector', 'bin')), may hold values from 0 to 255; in each aligned block of 1024 rows (0 to 1023, 1024 to 2047, ...) at most 8 rows name the same one
- body_list: int32 [256, 2], P(('sector', 'bin')), may hold values from 0 to 15, all different within a row
- tile_codes: int32 [256, 2, 32], P(('sector', 'bin')), may hold values from 0 to 511, as said below
- triangles: float32 [9, 16, 65536], P(None, 'sector', 'bin'), as said below
Outputs:
- new_state: float32 [7, 524288], P(None, ('sector', 'bin'))
- body_kick: float32 [16, 6], P('sector')
Inputs may be any that keep to these rules, and one draw needn't show every extreme that they name: `sph_dest`: within the spheres of one source bin no destination is named by more than 8 spheres, a bound that some block reaches. `body_list`: the 2 bodies of one bin are different. `tile_codes`: the 32 codes of one bin and intersection entry are different. `sph_state`: every radius (row 6) lies between 0.3 and 0.7. `triangles`: for every triangle, |e1 x e2|^2 is at least 0.2.
All inputs are finite; a program needn't handle non-finite values.
Results may differ from a plain program's by a relative error of at most 0.0003.
Values sent between devices are 32-bit elements; how exact they have to be, the bound alone decides.
A program may use at most 64 MiB of HBM per device.

v0:
```python
import jax
import jax.numpy as jnp
from jax import lax
from jax.sharding import PartitionSpec as P

stiff_pair = 50.0
damp_pair = 2.0
stiff_wall = 50.0
time_step = 0.01
gravity = 9.81
body_mass = 4.0
body_inertia = 40.0


def contact(spheres, facets):
    centre = spheres[0:3]
    radius = spheres[3]
    corner = facets[0:3]
    edge_one = facets[3:6] - corner
    edge_two = facets[6:9] - corner
    square_one = jnp.sum(edge_one * edge_one, 0)
    square_two = jnp.sum(edge_two * edge_two, 0)
    cross_term = jnp.sum(edge_one * edge_two, 0)
    inverse = 1.0 / (square_one * square_two - cross_term * cross_term)
    relative = centre[:, :, None] - corner[:, None, :]
    along_one = jnp.sum(relative * edge_one[:, None, :], 0)
    along_two = jnp.sum(relative * edge_two[:, None, :], 0)
    weight_b = (square_two * along_one - cross_term * along_two) * inverse
    weight_c = (square_one * along_two - cross_term * along_one) * inverse
    weight_a = jnp.maximum(1.0 - weight_b - weight_c, 0.0)
    weight_b = jnp.maximum(weight_b, 0.0)
    weight_c = jnp.maximum(weight_c, 0.0)
    totals = weight_a + weight_b + weight_c
    weight_b = weight_b / totals
    weight_c = weight_c / totals
    nearest = (
        corner[:, None, :]
        + weight_b[None] * edge_one[:, None, :]
        + weight_c[None] * edge_two[:, None, :]
    )
    offset = centre[:, :, None] - nearest
    squared = jnp.sum(offset * offset, 0)
    strength = stiff_wall * jnp.maximum(radius[:, None] * radius[:, None] - squared, 0.0)
    forces = strength[None] * offset
    on_spheres = jnp.sum(forces, 2)
    on_body = -jnp.sum(forces, (1, 2))
    torque = -jnp.sum(jnp.cross(nearest, forces, axis=0), (1, 2))
    return (on_spheres, jnp.concatenate([on_body, torque]))


def tile_forces(spheres, facets, tile_list):
    tiles_tri = facets.shape[1] // 128

    def advance_tile(carried, tile_code):
        forces, wrench = carried
        sphere_tile = tile_code // tiles_tri
        facet_tile = tile_code % tiles_tri
        sphere_part = lax.dynamic_slice_in_dim(spheres, sphere_tile * 128, 128, 1)
        facet_part = lax.dynamic_slice_in_dim(facets, facet_tile * 128, 128, 1)
        on_spheres, on_body = contact(sphere_part, facet_part)
        current = lax.dynamic_slice_in_dim(forces, sphere_tile * 128, 128, 1)
        forces = lax.dynamic_update_slice_in_dim(forces, current + on_spheres, sphere_tile * 128, 1)
        return ((forces, wrench + on_body), None)

    initial = (jnp.zeros((3, spheres.shape[1]), jnp.float32), jnp.zeros((6,), jnp.float32))
    (forces, wrench), unused = lax.scan(advance_tile, initial, tile_list)
    return (forces, wrench)


def sphere_forces(sphere_block):
    position = sphere_block[0:3]
    velocity = sphere_block[3:6]
    radius = sphere_block[6]
    width_all = sphere_block.shape[1]
    occupied = (radius > 0).astype(jnp.float32)
    coords = jnp.concatenate([position, radius[None]], 0)
    baseline = radius * radius - jnp.sum(position * position, 0)
    stacked = jnp.concatenate([position, velocity, jnp.ones((1, width_all), jnp.float32)], 0)
    row_block = 512

    def row_group(row_start):
        coords_rows = lax.dynamic_slice_in_dim(coords, row_start, row_block, 1)
        base_rows = lax.dynamic_slice_in_dim(baseline, row_start, row_block, 0)
        live_rows = lax.dynamic_slice_in_dim(occupied, row_start, row_block, 0)
        inner_products = lax.dot_general(
            coords_rows, coords, (((0,), (0,)), ((), ())), precision=lax.Precision.HIGHEST
        )
        intersection = jnp.maximum(
            base_rows[:, None] + baseline[None, :] + 2.0 * inner_products, 0.0
        )
        intersection = intersection * live_rows[:, None] * occupied[None, :]
        return lax.dot_general(
            stacked, intersection, (((1,), (1,)), ((), ())), precision=lax.Precision.HIGHEST
        )

    starts = jnp.arange(width_all // row_block, dtype=jnp.int32) * row_block
    grouped = lax.map(row_group, starts)
    weighted = jnp.transpose(grouped, (1, 0, 2)).reshape(7, width_all)
    totals = weighted[6]
    return stiff_pair * (totals * position - weighted[0:3]) - damp_pair * (
        totals * velocity - weighted[3:6]
    )


def advance(sphere_block, forces):
    position = sphere_block[0:3]
    velocity = sphere_block[3:6]
    radius = sphere_block[6]
    occupied = radius > 0
    masses = jnp.where(occupied, radius * radius * radius, 1.0)
    falling = jnp.array([0.0, 0.0, gravity], jnp.float32)
    acceleration = forces / masses[None] - falling[:, None]
    velocity_new = velocity + time_step * acceleration
    position_new = position + time_step * velocity_new
    result = jnp.concatenate([position_new, velocity_new, radius[None]], 0)
    return jnp.where(occupied[None], result, 0.0)


def bin_total(partial_row):
    return lax.psum(partial_row, "bin")


def local(sph_state, sph_dest, body_list, tile_codes, triangles):
    sectors = lax.axis_size("sector")
    bins = lax.axis_size("bin")
    ndevices = sectors * bins
    leaving = sph_state.shape[1]
    capacity = 2 * leaving // ndevices
    targets = sph_dest[:, 0]
    onehot = (targets[:, None] == jnp.arange(ndevices, dtype=jnp.int32)[None, :]).astype(jnp.int32)
    ranks = jnp.sum((jnp.cumsum(onehot, 0) - 1) * onehot, 1)
    columns = targets * capacity + ranks
    outgoing = jnp.zeros((7, ndevices * capacity), jnp.float32).at[:, columns].set(sph_state)
    outgoing = outgoing.reshape(7, sectors, bins, capacity)
    arrived = lax.all_to_all(
        lax.all_to_all(outgoing, "sector", split_axis=1, concat_axis=1, tiled=True),
        "bin",
        split_axis=2,
        concat_axis=2,
        tiled=True,
    )
    sphere_block = arrived.reshape(7, ndevices * capacity)
    width_all = sphere_block.shape[1]
    coords = jnp.concatenate([sphere_block[0:3], sphere_block[6:7]], 0)
    pair_total = sphere_forces(sphere_block)
    everyone = lax.all_gather(triangles, "sector", axis=1, tiled=True)
    wall_total = jnp.zeros((3, width_all), jnp.float32)
    partial_value = jnp.zeros((sectors, 6), jnp.float32)
    for slot_index in range(body_list.shape[1]):
        owner_body = body_list[0, slot_index]
        facets = lax.dynamic_index_in_dim(everyone, owner_body, 1, keepdims=False)
        on_spheres, on_body = tile_forces(coords, facets, tile_codes[0, slot_index])
        wall_total = wall_total + on_spheres
        selector = (jnp.arange(sectors, dtype=jnp.int32) == owner_body).astype(jnp.float32)
        partial_value = partial_value + selector[:, None] * on_body[None, :]
    own_row = lax.psum_scatter(partial_value, "sector", scatter_dimension=0, tiled=True)
    own_row = bin_total(own_row)
    new_block = advance(sphere_block, pair_total + wall_total)
    scaling = jnp.array([time_step / body_mass] * 3 + [time_step / body_inertia] * 3, jnp.float32)
    return (new_block, own_row * scaling[None, :])


def solution(mesh):
    return jax.shard_map(
        local,
        mesh=mesh,
        in_specs=(
            P(None, ("sector", "bin")),
            P(("sector", "bin"), None),
            P(("sector", "bin"), None),
            P(("sector", "bin"), None, None),
            P(None, "sector", "bin"),
        ),
        out_specs=(P(None, ("sector", "bin")), P("sector", None)),
        check_vma=False,
    )
```

profile of v0, /device:TPU:1, one launch (start us, length us, event | category | flops | bytes accessed | tf_op | source)
XLA Modules:
  0.0 446.5 jit_solution(9792508449313034145)
XLA Ops:
  7.2 0.8 copy.100
  9.4 3.3 scatter_custom_fusion
  12.7 0.9 copy.103
  13.7 0.8 reshape.697
  14.5 7.6 %all-to-all-start = ((f32[16,1,896]{2,1,0:T(1,128)}), f32[16,1,896]{2,1,0:T(1,128)S(1)}, u32[]{:S(2)}, u32[]{:S(2)}) async-start(f32[16,1,896]{2,1,0:T(1,128)} %reshape.697), calls=%async_computation | async-start | bytes 114688 | tf_op jit(solution)/shard_map/all_to_all | solution.py:136
  22.2 0.8 copy.110
  23.0 0.6 fusion.52
  23.6 1.2 compare_convert_fusion
  28.6 0.6 dynamic-slice
  29.7 0.8 reduce.1
  30.9 0.8 reshape.699
  31.7 10.0 %all-to-all-start.1 = ((f32[16,1,896]{2,1,0:T(1,128)}), f32[16,1,896]{2,1,0:T(1,128)S(1)}, u32[]{:S(2)}, u32[]{:S(2)}) async-start(f32[16,1,896]{2,1,0:T(1,128)} %reshape.699), calls=%async_computation.1 | async-start | bytes 114688 | tf_op jit(solution)/shard_map/all_to_all | solution.py:135
  41.7 7.6 %all-to-all-done.1 = f32[16,1,896]{2,1,0:T(1,128)S(1)} async-done(((f32[16,1,896]{2,1,0:T(1,128)}), f32[16,1,896]{2,1,0:T(1,128)S(1)}, u32[]{:S(2)}, u32[]{:S(2)}) %all-to-all-start.1) | async-done | bytes 57376 | tf_op jit(solution)/shard_map/all_to_all | solution.py:135
  49.4 0.8 reduce.2
  52.1 43.1 %while.40 = (s32[]{:T(128)}, f32[4,7,512]{2,1,0:T(8,128)S(1)}, s32[4]{0:T(128)S(1)}, f32[2048]{0:T(1024)S(1)}, f32[4,2048]{1,0:T(4,128)S(1)}, /*index=5*/f32[204...) while((s32[]{:T(128)}, f32[4,7,512]{2,1,0:T(8,128)S(1)}, s32[4]{0:T(128)S(1)}, ...), condition=%wide.region_6.7_spmd, body=%wide.region_5.6_spmd.sunk | while | flops 144703488 | bytes 8540331 | solution.py:97
  52.1 0.6 dynamic_slice.98
  54.6 3.6 fusion.71
  58.3 4.5 %fusion.72 = f32[4,7,512]{2,1,0:T(8,128)S(1)} fusion(f32[4,7,512]{2,1,0:T(8,128)S(1)} %get-tuple-element.710, s32[]{:T(128)S(6)} %copy.137, f32[7,2048]{1,0:T(8,128)S(1)} %get-tuple-element.725, f32[512,2048]{1,0:T(8,128)S(1)} %fusion.71, f32[2048]{0:T(1024)S(1)} %get-tuple-element.724, f32[512]{0:T(512)S(1)} %dynamic_slice.99, ...), kind=kOutput, calls=%fused_computation.15.clone.1 | convolution fusion | flops 94371840 | bytes 4296708 | tf_op jit(solution)/shard_map/while/body/eval_jaxpr/dot_general | solution.py:92
  62.8 0.6 dynamic_slice.98
  65.4 3.6 fusion.71
  69.1 4.5 %fusion.72 = f32[4,7,512]{2,1,0:T(8,128)S(1)} fusion(f32[4,7,512]{2,1,0:T(8,128)S(1)} %get-tuple-element.710, s32[]{:T(128)S(6)} %copy.137, f32[7,2048]{1,0:T(8,128)S(1)} %get-tuple-element.725, f32[512,2048]{1,0:T(8,128)S(1)} %fusion.71, f32[2048]{0:T(1024)S(1)} %get-tuple-element.724, f32[512]{0:T(512)S(1)} %dynamic_slice.99, ...), kind=kOutput, calls=%fused_computation.15.clone.1 | convolution fusion | flops 94371840 | bytes 4296708 | tf_op jit(solution)/shard_map/while/body/eval_jaxpr/dot_general | solution.py:92
  73.6 0.6 dynamic_slice.98
  76.1 3.6 fusion.71
  79.9 4.5 %fusion.72 = f32[4,7,512]{2,1,0:T(8,128)S(1)} fusion(f32[4,7,512]{2,1,0:T(8,128)S(1)} %get-tuple-element.710, s32[]{:T(128)S(6)} %copy.137, f32[7,2048]{1,0:T(8,128)S(1)} %get-tuple-element.725, f32[512,2048]{1,0:T(8,128)S(1)} %fusion.71, f32[2048]{0:T(1024)S(1)} %get-tuple-element.724, f32[512]{0:T(512)S(1)} %dynamic_slice.99, ...), kind=kOutput, calls=%fused_computation.15.clone.1 | convolution fusion | flops 94371840 | bytes 4296708 | tf_op jit(solution)/shard_map/while/body/eval_jaxpr/dot_general | solution.py:92
  84.4 0.6 dynamic_slice.98
  86.9 3.6 fusion.71
  90.7 4.5 %fusion.72 = f32[4,7,512]{2,1,0:T(8,128)S(1)} fusion(f32[4,7,512]{2,1,0:T(8,128)S(1)} %get-tuple-element.710, s32[]{:T(128)S(6)} %copy.137, f32[7,2048]{1,0:T(8,128)S(1)} %get-tuple-element.725, f32[512,2048]{1,0:T(8,128)S(1)} %fusion.71, f32[2048]{0:T(1024)S(1)} %get-tuple-element.724, f32[512]{0:T(512)S(1)} %dynamic_slice.99, ...), kind=kOutput, calls=%fused_computation.15.clone.1 | convolution fusion | flops 94371840 | bytes 4296708 | tf_op jit(solution)/shard_map/while/body/eval_jaxpr/dot_general | solution.py:92
  95.2 1.1 dynamic-slice_bitcast_fusion
  96.3 138.3 %while.41 = (s32[]{:T(128)}, f32[3,2048]{1,0:T(4,128)S(1)}, f32[6]{0:T(128)S(1)}, s32[32]{0:T(128)S(1)}, f32[4,2048]{1,0:T(4,128)S(1)}, /*index=5*/f32[9,4096]{1...) while((s32[]{:T(128)}, f32[3,2048]{1,0:T(4,128)S(1)}, ...), condition=%wide.region_17.19_spmd.clone, body=%wide.region_7.18_spmd.clone.sunk | while | flops 1559858 | bytes 2144398 | solution.py:66
  96.3 0.6 dynamic_slice.103
  100.7 0.6 dynamic_slice.103
  105.0 0.6 dynamic_slice.103
  113.6 0.6 dynamic_slice.103
  117.9 0.6 dynamic_slice.103
  126.6 0.6 dynamic_slice.103
  130.9 0.6 dynamic_slice.103
  143.9 0.6 dynamic_slice.103
  156.8 0.6 dynamic_slice.103
  161.1 0.6 dynamic_slice.103
  169.8 0.6 dynamic_slice.103
  174.1 0.6 dynamic_slice.103
  182.7 0.6 dynamic_slice.103
  187.1 0.6 dynamic_slice.103
  234.6 138.3 %while.42 = (s32[]{:T(128)}, f32[3,2048]{1,0:T(4,128)S(1)}, f32[6]{0:T(128)S(1)}, s32[32]{0:T(128)S(1)}, f32[4,2048]{1,0:T(4,128)S(1)}, /*index=5*/f32[9,4096]{1...) while((s32[]{:T(128)}, f32[3,2048]{1,0:T(4,128)S(1)}, ...), condition=%wide.region_28.30_spmd.clone, body=%wide.region_18.29_spmd.clone.sunk | while | flops 1559858 | bytes 2144398 | solution.py:66
  234.6 0.6 dynamic_slice.106
  373.9 33.5 %all-reduce = f32[16,6]{1,0:T(8,128)S(1)} all-reduce(f32[16,6]{1,0:T(8,128)S(1)} %copy.112), channel_id=2, replica_groups=mesh['sector'=16,'bin'=16] {'sector'}, use_global_device_ids=true, to_apply=%region_29.31.clone | all-reduce | flops 96 | bytes 768
  407.9 1.0 copy.113
  408.9 30.3 %psum.7 = f32[1,6]{1,0:T(1,128)S(1)} all-reduce(f32[1,6]{1,0:T(1,128)S(1)} %constant_dynamic-slice_fusion.4), channel_id=1, replica_groups=mesh['sector'=16,'bin'=16] {'bin'}, use_global_device_ids=true, to_apply=%region_30.32 | all-reduce | flops 6 | bytes 48 | tf_op jit(solution)/shard_map/psum | solution.py:120
  (1083 shorter events, 103.0 us)
Async XLA Ops:
  7.2 1.6 copy-start.1
  7.2 2.0 copy-start.2
  8.3 13.9 %copy-start = (f32[9,1,4096]{2,1,0:T(1,128)S(1)}, f32[9,1,4096]{2,1,0:T(1,128)}, u32[]{:S(2)}) copy-start(f32[9,1,4096]{2,1,0:T(1,128)} %param.19) | copy-start | bytes 442372
  8.4 14.6 %copy-start.4 = (s32[1,2,32]{2,1,0:T(2,128)S(1)}, s32[1,2,32]{2,1,0:T(2,128)}, u32[]{:S(2)}) copy-start(s32[1,2,32]{2,1,0:T(2,128)} %param.18) | copy-start | bytes 772
  8.4 14.6 %copy-start.3 = (s32[1,2]{1,0:T(1,128)S(1)}, s32[1,2]{1,0:T(1,128)}, u32[]{:S(2)}) copy-start(s32[1,2]{1,0:T(1,128)} %param.17) | copy-start | bytes 28
  8.4 20.2 %copy-start.6 = (u32[256]{0:T(256)S(1)}, u32[256]{0:T(256)}, u32[]{:S(2)}) copy-start(u32[256]{0:T(256)} %constant.228) | copy-start | bytes 3076
  14.5 14.7 %all-to-all-start = ((f32[16,1,896]{2,1,0:T(1,128)}), f32[16,1,896]{2,1,0:T(1,128)S(1)}, u32[]{:S(2)}, u32[]{:S(2)}) async-start(f32[16,1,896]{2,1,0:T(1,128)} %reshape.697), calls=%async_computation | async-start | bytes 114688 | tf_op jit(solution)/shard_map/all_to_all | solution.py:136
  22.1 73.1 %all-gather.2.cloned.1.call-start = ((), (), s32[]{:S(2)}) async-start(), calls=%async_computation.2 | async-start | bytes 4456448 | tf_op jit(solution)/shard_map/all_gather | solution.py:146
  31.7 17.6 %all-to-all-start.1 = ((f32[16,1,896]{2,1,0:T(1,128)}), f32[16,1,896]{2,1,0:T(1,128)S(1)}, u32[]{:S(2)}, u32[]{:S(2)}) async-start(f32[16,1,896]{2,1,0:T(1,128)} %reshape.699), calls=%async_computation.1 | async-start | bytes 114688 | tf_op jit(solution)/shard_map/all_to_all | solution.py:135
  234.6 138.3 %copy-start.5 = (f32[3]{0:T(128)S(1)}, f32[3]{0:T(128)}, u32[]{:S(2)}) copy-start(f32[3]{0:T(128)} %constant.224) | copy-start | bytes 40
  372.9 66.3 %copy-start.7 = (f32[1,6]{1,0:T(1,128)S(1)}, f32[1,6]{1,0:T(1,128)}, u32[]{:S(2)}) copy-start(f32[1,6]{1,0:T(1,128)} %constant.225) | copy-start | bytes 76
Sparse Core Ops, SparseCore 0:
  25.4 60.0 all-gather.1
where the time goes:
time: 451 us; the launch traced here: 447 us
  loops' own time  180 us (40%)
  other arithmetic  71.6 us (16%)
  blocking collectives  63.7 us (14%)
  local copies, waits for them, and re-layouts  56 us (12%)
  matrix products  32.3 us (7%)
  between operations  18.1 us (4%)
  starting transfers between devices  17.6 us (4%)
  waiting for transfers between devices  7.67 us (2%)
    another operation x2, loops' own time, tile_forces(): (forces, wrench), unused = lax.scan(advance_tile, initial, tile_list)  172 us
    dynamic_slice x64, local copies, waits for them, and re-layouts, tile_forces(): (forces, wrench), unused = lax.scan(advance_tile, initial, tile_list)  37.3 us
    unnamed x1, blocking collectives  33.5 us
    psum x1, blocking collectives, bin_total(): return lax.psum(partial_row, 'bin')  30.3 us
    reduce_sum x64, other arithmetic, contact(): on_body = -jnp.sum(forces, (1, 2))  19.1 us
    dot_general x4, matrix products, row_group(): lax.dot_general(stacked, intersection, (((1,), (1,)), ((), ())), precisio...  17.9 us
    dot_general x4, matrix products, row_group(): lax.dot_general(coords_rows, coords, (((0,), (0,)), ((), ())), precision=...  14.3 us
    all_to_all x1, starting transfers between devices, local(): lax.all_to_all(lax.all_to_all(outgoing, 'sector', split_axis=1, concat_ax...  9.99 us
  transfers between devices with their start and end apart: 3, of which 1 were waited for; matrix products, arithmetic and copies ran while one was open for 10% of the time, Pallas kernels for 0%

commit v1 on v0

v1 whole, which is shorter than its diff:
```python
import functools

import jax
import jax.numpy as jnp
from jax import lax
from jax.experimental import pallas as pl
from jax.experimental.pallas import tpu as pltpu
from jax.sharding import PartitionSpec as P

stiff_pair = 50.0
damp_pair = 2.0
stiff_wall = 50.0
time_step = 0.01
gravity = 9.81
body_mass = 4.0
body_inertia = 40.0

MESH = pl.DeviceIdType.MESH
N = 16
HOLDERS = 12
f32, bf16, i32 = jnp.float32, jnp.bfloat16, jnp.int32


def split3(value):
    high = value.astype(bf16).astype(f32)
    rest = value - high
    middle = rest.astype(bf16).astype(f32)
    return high, middle, rest - middle


def is_holder(s):
    return (s // 4) != (s % 4)


def piece_of(s):
    y, x = s // 4, s % 4
    return 3 * y + x - jnp.where(x > y, 1, 0)


def holder_at(piece):
    y, x = piece // 3, piece % 3
    return 4 * y + x + (1 if x >= y else 0)


def greet(sector, bin_):
    barrier = pltpu.get_barrier_semaphore()
    for off in range(1, N):
        pl.semaphore_signal(barrier, inc=1, device_id=(sector, lax.rem(bin_ + off, N)), device_id_type=MESH)
        pl.semaphore_signal(barrier, inc=1, device_id=(lax.rem(sector + off, N), bin_), device_id_type=MESH)
    return barrier


def outgoing_tiles(state_ref, dest_ref, out_ref):
    leaving = state_ref.shape[1]
    dest = dest_ref[...]
    width = 256
    row = lax.broadcasted_iota(i32, (256, width), 0)
    before = (row < lax.broadcasted_iota(i32, (256, width), 1)).astype(bf16)
    counting = jnp.concatenate([before, jnp.ones((256, width), bf16)], 1)
    carry = jnp.zeros((256, width), f32)
    ranks = []
    for part in range(leaving // width):
        hit = row == dest[:, part * width : (part + 1) * width]
        counted = jnp.dot(hit.astype(bf16), counting, preferred_element_type=f32)
        ranks.append(jnp.sum(jnp.where(hit, counted[:, :width] + carry, 0.0), 0, keepdims=True))
        carry = carry + counted[:, width:]
    rank = jnp.concatenate(ranks, 1).astype(i32)
    key = (dest // N) * 8 + rank
    picks = (lax.broadcasted_iota(i32, (128, leaving), 0) == key).astype(bf16)
    state = state_ref[...]
    state = jnp.concatenate([state, jnp.zeros((1, leaving), f32)], 0)
    stacked = jnp.concatenate(split3(state), 0)
    lane_bin = dest % N
    chosen = [jnp.where(lane_bin == db, stacked, 0.0) for db in range(N)]
    chosen = jnp.concatenate(chosen, 0).astype(bf16)
    placed = lax.dot_general(chosen, picks, (((1,), (1,)), ((), ())), preferred_element_type=f32)
    for db in range(N):
        base = 24 * db
        out_ref[db] = placed[base : base + 8] + placed[base + 8 : base + 16] + placed[base + 16 : base + 24]


def swap_groups(tiles):
    lane = lax.broadcasted_iota(i32, (8, 128), 1)
    for bit in (1, 2, 4, 8):
        low = (lane // 8) % (2 * bit) < bit
        fresh = list(tiles)
        for a in range(N):
            if a & bit == 0:
                b = a | bit
                fresh[a] = jnp.where(low, tiles[a], pltpu.roll(tiles[b], 8 * bit, 1))
                fresh[b] = jnp.where(low, pltpu.roll(tiles[a], 128 - 8 * bit, 1), tiles[b])
        tiles = fresh
    return tiles


def exchange_kernel(
    state_ref, dest_ref, body_ref, tri_ref, sph_out, sel_out,
    out1, got1, out2, got2, piece, sel_send, sel_got, names, names_got, names_smem,
    s1, r1, s2, r2, t1s, t1r, ns, nr, t2s, t2r, own_sem, names_sem,
):
    sector, bin_ = lax.axis_index("sector"), lax.axis_index("bin")
    barrier = greet(sector, bin_)
    outgoing_tiles(state_ref, dest_ref, out1)
    lane = lax.broadcasted_iota(i32, (1, 128), 1)
    names[...] = jnp.where(lane == 0, body_ref[0, 0], body_ref[0, 1])
    pl.semaphore_wait(barrier, 2 * (N - 1))

    def sphere_one(src, dst):
        return pltpu.make_async_remote_copy(
            src_ref=out1.at[dst], dst_ref=got1.at[src], send_sem=s1.at[dst], recv_sem=r1.at[src],
            device_id=(sector, dst), device_id_type=MESH,
        )

    def sphere_two(src, dst):
        return pltpu.make_async_remote_copy(
            src_ref=out2.at[dst], dst_ref=got2.at[src], send_sem=s2.at[dst], recv_sem=r2.at[src],
            device_id=(dst, bin_), device_id_type=MESH,
        )

    def piece_one(src, dst):
        return pltpu.make_async_remote_copy(
            src_ref=tri_ref.at[pl.ds(3 * piece_of(dst), 3)], dst_ref=piece.at[src], send_sem=t1s.at[dst], recv_sem=t1r.at[src],
            device_id=(dst, bin_), device_id_type=MESH,
        )

    def names_one(src, dst):
        return pltpu.make_async_remote_copy(
            src_ref=names, dst_ref=names_got.at[src], send_sem=ns.at[dst], recv_sem=nr.at[src],
            device_id=(dst, bin_), device_id_type=MESH,
        )

    def piece_two(src, dst):
        return pltpu.make_async_remote_copy(
            src_ref=sel_send.at[dst], dst_ref=sel_got.at[piece_of(src)], send_sem=t2s.at[dst], recv_sem=t2r.at[src],
            device_id=(dst, bin_), device_id_type=MESH,
        )

    def peers(me):
        return [lax.rem(me + off, N) for off in range(1, N)]

    holding = is_holder(sector)
    for peer in peers(bin_):
        sphere_one(bin_, peer).start()
    for peer in peers(sector):

        @pl.when(is_holder(peer))
        def _(peer=peer):
            piece_one(sector, peer).start()
            names_one(sector, peer).start()

    @pl.when(holding)
    def _():
        own = pltpu.make_async_copy(tri_ref.at[pl.ds(3 * piece_of(sector), 3)], piece.at[sector], own_sem)
        own.start()
        names_got[sector] = names[...]
        own.wait()

    got1[bin_] = out1[bin_]
    for peer in peers(bin_):
        sphere_one(peer, bin_).wait_recv()
    for ds, tile in enumerate(swap_groups([got1[sb] for sb in range(N)])):
        out2[ds] = tile
    for peer in peers(sector):
        sphere_two(sector, peer).start()
    got2[sector] = out2[sector]

    @pl.when(holding)
    def _():
        for peer in peers(sector):
            names_one(peer, sector).wait_recv()
        listed = pltpu.make_async_copy(names_got, names_smem, names_sem)
        listed.start()
        for peer in peers(sector):
            piece_one(peer, sector).wait_recv()
        listed.wait()
        for dst in range(N):
            for entry in range(2):
                sel_send[dst, entry] = piece[names_smem[dst, 0, entry]]
        for peer in peers(sector):
            piece_two(sector, peer).start()
        sel_got[piece_of(sector)] = sel_send[sector]

    for peer in peers(sector):
        sphere_two(peer, sector).wait_recv()
    for ss in range(N):
        sph_out[ss] = got2[ss]
    for peer in peers(sector):

        @pl.when(is_holder(peer))
        def _(peer=peer):
            piece_two(peer, sector).wait_recv()

    for p in range(HOLDERS):
        sel_out[p] = sel_got[p]

    for peer in peers(bin_):
        sphere_one(bin_, peer).wait_send()
    for peer in peers(sector):
        sphere_two(sector, peer).wait_send()

        @pl.when(is_holder(peer))
        def _(peer=peer):
            piece_one(sector, peer).wait_send()
            names_one(sector, peer).wait_send()

    @pl.when(holding)
    def _():
        for peer in peers(sector):
            piece_two(sector, peer).wait_send()


def exchange(state, dest, bodies, tri):
    dma = pltpu.SemaphoreType.DMA
    return pl.pallas_call(
        exchange_kernel,
        out_shape=(
            jax.ShapeDtypeStruct((N, 8, 128), f32),
            jax.ShapeDtypeStruct((HOLDERS, 2, 3, 8, 128), f32),
        ),
        in_specs=[
            pl.BlockSpec(memory_space=pltpu.VMEM),
            pl.BlockSpec(memory_space=pltpu.VMEM),
            pl.BlockSpec(memory_space=pltpu.SMEM),
            pl.BlockSpec(memory_space=pl.ANY),
        ],
        out_specs=(pl.BlockSpec(memory_space=pltpu.VMEM), pl.BlockSpec(memory_space=pltpu.VMEM)),
        scratch_shapes=[
            pltpu.VMEM((N, 8, 128), f32),
            pltpu.VMEM((N, 8, 128), f32),
            pltpu.VMEM((N, 8, 128), f32),
            pltpu.VMEM((N, 8, 128), f32),
            pltpu.VMEM((N, 3, 8, 128), f32),
            pltpu.VMEM((N, 2, 3, 8, 128), f32),
            pltpu.VMEM((HOLDERS, 2, 3, 8, 128), f32),
            pltpu.VMEM((1, 128), i32),
            pltpu.VMEM((N, 1, 128), i32),
            pltpu.SMEM((N, 1, 128), i32),
        ]
        + [dma((N,))] * 10
        + [dma, dma],
        compiler_params=pltpu.CompilerParams(
            collective_id=0, has_side_effects=True, vmem_limit_bytes=32 * 2**20
        ),
    )(state, dest, bodies, tri)


def pair_features(sph):
    width = sph.shape[1]
    position, radius = sph[0:3], sph[6:7]
    base = radius * radius - jnp.sum(position * position, 0, keepdims=True)
    base = jnp.where(radius > 0, base, -1e30)
    high, middle, low = split3(jnp.concatenate([position, radius], 0))
    base = jnp.concatenate(split3(base), 0)
    one = jnp.ones((3, width), f32)
    none = jnp.zeros((2, width), f32)
    left = [2.0 * high, 2.0 * high, 2.0 * middle, 2.0 * middle, 2.0 * high, 2.0 * low, base, one, none]
    right = [high, middle, high, middle, low, high, one, base, none]
    row = lax.broadcasted_iota(i32, sph.shape, 0)
    weighed = jnp.where(row == 6, 1.0, sph)
    high, middle, low = split3(weighed)
    stacked = jnp.concatenate([high, middle, low, jnp.zeros_like(high)], 0)
    return (
        jnp.concatenate(left, 0).astype(bf16),
        jnp.concatenate(right, 0).astype(bf16),
        stacked.astype(bf16),
    )


def triangle_features(corner):
    a, e1, e2 = corner[0:3], [corner[3 + k] - corner[k] for k in range(3)], [corner[6 + k] - corner[k] for k in range(3)]
    d11 = e1[0] * e1[0] + e1[1] * e1[1] + e1[2] * e1[2]
    d12 = e1[0] * e2[0] + e1[1] * e2[1] + e1[2] * e2[2]
    d22 = e2[0] * e2[0] + e2[1] * e2[1] + e2[2] * e2[2]
    inverse = 1.0 / (d11 * d22 - d12 * d12)
    for_b = [(d22 * e1[k] - d12 * e2[k]) * inverse for k in range(3)]
    for_c = [(d11 * e2[k] - d12 * e1[k]) * inverse for k in range(3)]
    return [*a, *e1, *e2, *for_b, *for_c]


def contact_kernel(
    code_ref, body_ref, sph_ref, sel_ref, state_out, part_out,
    wide, feat, acc, left_ref, stacked_ref, summed,
):
    tiles = sph_ref.shape[0]
    entries = code_ref.shape[0]
    sph = jnp.concatenate([sph_ref[t] for t in range(tiles)], 1)

    left, right, stacked = pair_features(sph)
    left_ref[...] = left
    stacked_ref[...] = stacked
    summed[...] = jnp.zeros_like(summed)
    rows = 256

    def row_group(step, carry):
        start = pl.multiple_of(step * rows, rows)
        gap = lax.dot_general(
            left_ref[:, pl.ds(start, rows)], right, (((0,), (0,)), ((), ())), preferred_element_type=f32
        )
        inter = jnp.maximum(gap, 0.0)
        high = inter.astype(bf16)
        low = (inter - high.astype(f32)).astype(bf16)
        weighed = stacked_ref[:, pl.ds(start, rows)]
        summed[...] += jnp.dot(weighed, high, preferred_element_type=f32) + jnp.dot(
            weighed, low, preferred_element_type=f32
        )
        return carry

    lax.fori_loop(0, tiles * 128 // rows, row_group, 0)

    for entry in range(entries):
        for group in range(4):
            corner = []
            for c in range(9):
                at = c * 4 + group
                corner.append(sel_ref[at // 3, entry, at % 3])
            for f, value in enumerate(triangle_features(corner)):
                feat[entry, f, pl.ds(8 * group, 8), :] = value
    for t in range(tiles):
        turned = sph_ref[t].T
        for f, c in enumerate((0, 1, 2, 6)):
            column = turned[:, c : c + 1]
            if c == 6:
                column = column * column
            wide[f, pl.ds(128 * t, 128), :] = jnp.broadcast_to(column, (128, 128))
    acc[...] = jnp.zeros_like(acc)
    for entry in range(entries):

        def tile_pair(step, carry, entry=entry):
            code = code_ref[entry, step]
            st, tt = code // 32, code % 32
            ax, ay, az, ux, uy, uz, wx, wy, wz, bx, by, bz, cx, cy, cz = (
                jnp.broadcast_to(feat[entry, f, pl.ds(tt, 1), :], (8, 128)) for f in range(15)
            )
            for group in range(16):
                at = pl.ds(pl.multiple_of(st * 128 + 8 * group, 8), 8)
                dx, dy, dz = wide[0, at, :] - ax, wide[1, at, :] - ay, wide[2, at, :] - az
                b = bx * dx + by * dy + bz * dz
                c = cx * dx + cy * dy + cz * dz
                a = jnp.maximum((1.0 - b) - c, 0.0)
                b = jnp.maximum(b, 0.0)
                c = jnp.maximum(c, 0.0)
                total = a + b + c
                inverse = pl.reciprocal(total, approx=True)
                inverse = inverse * (2.0 - total * inverse)
                b, c = b * inverse, c * inverse
                ox = dx - b * ux - c * wx
                oy = dy - b * uy - c * wy
                oz = dz - b * uz - c * wz
                strength = jnp.maximum(wide[3, at, :] - (ox * ox + oy * oy + oz * oz), 0.0)
                here = pl.ds(8 * group, 8)
                acc[entry, st, 0, here, :] += strength * ox
                acc[entry, st, 1, here, :] += strength * oy
                acc[entry, st, 2, here, :] += strength * oz
            return carry

        lax.fori_loop(0, code_ref.shape[1], tile_pair, 0)

    summed_all = summed[...]
    weighted = summed_all[0:8] + summed_all[8:16] + summed_all[16:24]
    ones = jnp.ones((16, 128), bf16)
    wrench = [[jnp.zeros((1, 128), f32)] * 6 for _ in range(entries)]
    for t in range(tiles):
        lanes = slice(128 * t, 128 * t + 128)
        tile = sph_ref[t]
        pos, vel, radius = [tile[k : k + 1] for k in range(3)], [tile[3 + k : 4 + k] for k in range(3)], tile[6:7]
        wall = [jnp.zeros((1, 128), f32)] * 3
        for entry in range(entries):
            force = []
            for k in range(3):
                block = acc[entry, t, k]
                high = block.astype(bf16)
                low = (block - high.astype(f32)).astype(bf16)
                dims = (((1,), (1,)), ((), ()))
                total = lax.dot_general(ones, high, dims, preferred_element_type=f32) + lax.dot_general(
                    ones, low, dims, preferred_element_type=f32
                )
                force.append(stiff_wall * total[0:1])
            wall = [wall[k] + force[k] for k in range(3)]
            moment = [
                pos[1] * force[2] - pos[2] * force[1],
                pos[2] * force[0] - pos[0] * force[2],
                pos[0] * force[1] - pos[1] * force[0],
            ]
            wrench[entry] = [w - f for w, f in zip(wrench[entry], force + moment)]
        live = radius > 0
        mass = jnp.where(live, radius * radius * radius, 1.0)
        totals = weighted[6:7, lanes]
        out_pos, out_vel = [], []
        for k in range(3):
            pair = stiff_pair * (totals * pos[k] - weighted[k : k + 1, lanes]) - damp_pair * (
                totals * vel[k] - weighted[3 + k : 4 + k, lanes]
            )
            acceleration = (pair + wall[k]) / mass - (gravity if k == 2 else 0.0)
            fresh = vel[k] + time_step * acceleration
            out_vel.append(fresh)
            out_pos.append(pos[k] + time_step * fresh)
        block = jnp.concatenate([*out_pos, *out_vel, radius], 0)
        state_out[:, lanes] = jnp.where(live, block, 0.0)

    lane = lax.broadcasted_iota(i32, (1, 128), 1)
    row = lax.broadcasted_iota(i32, (N, 1, 128), 0)
    part = jnp.zeros((N, 1, 128), f32)
    for entry in range(entries):
        line = jnp.zeros((1, 128), f32)
        for k in range(6):
            line = jnp.where(lane == k, jnp.sum(wrench[entry][k], 1, keepdims=True), line)
        part = part + jnp.where(row == body_ref[0, entry], line[None], 0.0)
    part_out[...] = part


def contacts(codes, bodies, sph, sel):
    slots = sph.shape[0] * 128
    smem, vmem = pl.BlockSpec(memory_space=pltpu.SMEM), pl.BlockSpec(memory_space=pltpu.VMEM)
    return pl.pallas_call(
        contact_kernel,
        out_shape=(jax.ShapeDtypeStruct((7, slots), f32), jax.ShapeDtypeStruct((N, 1, 128), f32)),
        in_specs=[smem, smem, vmem, vmem],
        out_specs=(vmem, vmem),
        scratch_shapes=[
            pltpu.VMEM((4, slots, 128), f32),
            pltpu.VMEM((2, 15, 32, 128), f32),
            pltpu.VMEM((2, sph.shape[0], 3, 128, 128), f32),
            pltpu.VMEM((32, slots), bf16),
            pltpu.VMEM((32, slots), bf16),
            pltpu.VMEM((32, slots), f32),
        ],
        compiler_params=pltpu.CompilerParams(vmem_limit_bytes=48 * 2**20),
    )(codes, bodies, sph, sel)


def wrench_kernel(part_ref, out_ref, sent, got1, row, got2, s1, r1, s2, r2):
    sector, bin_ = lax.axis_index("sector"), lax.axis_index("bin")
    barrier = greet(sector, bin_)
    for k in range(N):
        sent[k] = part_ref[k]
    pl.semaphore_wait(barrier, 2 * (N - 1))

    def one(src, dst):
        return pltpu.make_async_remote_copy(
            src_ref=sent.at[dst], dst_ref=got1.at[src], send_sem=s1.at[dst], recv_sem=r1.at[src],
            device_id=(dst, bin_), device_id_type=MESH,
        )

    def two(src, dst):
        return pltpu.make_async_remote_copy(
            src_ref=row, dst_ref=got2.at[src], send_sem=s2.at[dst], recv_sem=r2.at[src],
            device_id=(sector, dst), device_id_type=MESH,
        )

    def peers(me):
        return [lax.rem(me + off, N) for off in range(1, N)]

    for peer in peers(sector):
        one(sector, peer).start()
    got1[sector] = sent[sector]
    for peer in peers(sector):
        one(peer, sector).wait_recv()
    row[...] = functools.reduce(jnp.add, [got1[k] for k in range(N)])
    for peer in peers(bin_):
        two(bin_, peer).start()
    got2[bin_] = row[...]
    for peer in peers(bin_):
        two(peer, bin_).wait_recv()
    total = functools.reduce(jnp.add, [got2[k] for k in range(N)])
    lane = lax.broadcasted_iota(i32, (1, 128), 1)
    total = total * jnp.where(lane < 3, time_step / body_mass, time_step / body_inertia)
    out_ref[...] = total[:, 0:6]
    for peer in peers(sector):
        one(sector, peer).wait_send()
    for peer in peers(bin_):
        two(bin_, peer).wait_send()


def wrench_sum(part):
    dma = pltpu.SemaphoreType.DMA
    line = pltpu.VMEM((N, 1, 128), f32)
    return pl.pallas_call(
        wrench_kernel,
        out_shape=jax.ShapeDtypeStruct((1, 6), f32),
        in_specs=[pl.BlockSpec(memory_space=pltpu.VMEM)],
        out_specs=pl.BlockSpec(memory_space=pltpu.VMEM),
        scratch_shapes=[line, line, pltpu.VMEM((1, 128), f32), line] + [dma((N,))] * 4,
        compiler_params=pltpu.CompilerParams(collective_id=1, has_side_effects=True),
    )(part)


def local(sph_state, sph_dest, body_list, tile_codes, triangles):
    dest = sph_dest.reshape(1, -1)
    tri = triangles.reshape(36, 8, 128)
    sph, sel = exchange(sph_state, dest, body_list, tri)
    new_block, part = contacts(tile_codes[0], body_list, sph, sel)
    return new_block, wrench_sum(part)


def solution(mesh):
    return jax.shard_map(
        local,
        mesh=mesh,
        in_specs=(
            P(None, ("sector", "bin")),
            P(("sector", "bin"), None),
            P(("sector", "bin"), None),
            P(("sector", "bin"), None, None),
            P(None, "sector", "bin"),
        ),
        out_specs=(P(None, ("sector", "bin")), P("sector", None)),
        check_vma=False,
    )
```

time: 451 us -> 67.9 us (0.15)
  loops' own time: 180 us -> 0 us
  other arithmetic: 71.6 us -> 0 us
  blocking collectives: 63.7 us -> 0 us
  Pallas kernels: 0 us -> 62.2 us
  local copies, waits for them, and re-layouts: 56 us -> 4.79 us
  matrix products: 32.3 us -> 0 us
  starting transfers between devices: 17.6 us -> 0 us
  between operations: 18.1 us -> 0.68 us
  waiting for transfers between devices: 7.67 us -> 0 us
    another operation x3 -> x0, loops' own time: 180 us -> none  [the longest x2 172 us: tile_forces(): (forces, wrench), unused = lax.scan(advance_tile, initial, tile_list)]
    pallas_call x0 -> x3, Pallas kernels: none -> 62.2 us  [the longest x1 25.4 us: exchange(): pl.pallas_call(exchange_kernel, out_shape=(jax.ShapeDtypeStruct((N, 8, 12...]
    reduce_sum x322 -> x0, other arithmetic: 49.3 us -> none  [the longest x64 19.1 us: contact(): on_body = -jnp.sum(forces, (1, 2))]
    dynamic_slice x140 -> x0, local copies, waits for them, and re-layouts: 40.9 us -> none  [the longest x64 37.3 us: tile_forces(): (forces, wrench), unused = lax.scan(advance_tile, initial, tile_list)]
    unnamed x1 -> x0, blocking collectives: 33.5 us -> none
    dot_general x8 -> x0, matrix products: 32.3 us -> none  [the longest x4 17.9 us: row_group(): lax.dot_general(stacked, intersection, (((1,), (1,)), ((), ())), precisio...]
    psum x1 -> x0, blocking collectives: 30.3 us -> none  [bin_total(): return lax.psum(partial_row, 'bin')]
    all_to_all x2 -> x0, starting transfers between devices: 17.6 us -> none  [the longest x1 9.99 us: local(): lax.all_to_all(lax.all_to_all(outgoing, 'sector', split_axis=1, concat_ax...]
  transfers between devices with their start and end apart: 3 -> 0, of which waited for: 1 -> 0; matrix products, arithmetic and copies ran while one was open for 10% -> 0% of each run, Pallas kernels for 0% -> 0%
where the time goes in v1:
time: 67.9 us; the launch traced here: 67.6 us
  Pallas kernels  62.2 us (92%)
  local copies, waits for them, and re-layouts  4.79 us (7%)
  between operations  0.68 us (1%)
    pallas_call x1, Pallas kernels, exchange(): pl.pallas_call(exchange_kernel, out_shape=(jax.ShapeDtypeStruct((N, 8, 12...  25.4 us
    pallas_call x1, Pallas kernels, contacts(): pl.pallas_call(contact_kernel, out_shape=(jax.ShapeDtypeStruct((7, slots)...  21.7 us
    pallas_call x1, Pallas kernels, wrench_sum(): pl.pallas_call(wrench_kernel, out_shape=jax.ShapeDtypeStruct((1, 6), f32)...  15 us
    unnamed x13, local copies, waits for them, and re-layouts  4.79 us

profile of v1, /device:TPU:1, one launch (start us, length us, event | category | flops | bytes accessed | tf_op | source)
XLA Modules:
  0.0 67.6 jit_solution(14621696958142456554)
XLA Ops:
  0.6 0.0 copy-start.3
  0.6 0.0 copy-start.4
  0.7 0.7 copy-done.3
  1.3 0.0 copy-done.4
  1.3 0.0 copy-start
  1.3 0.9 %copy-done = f32[9,1,4096]{2,1,0:T(1,128)S(1)} copy-done((f32[9,1,4096]{2,1,0:T(1,128)S(1)}, f32[9,1,4096]{2,1,0:T(1,128)}, u32[]{:S(2)}) %copy-start) | copy-done | bytes 147480
  2.2 0.0 copy-start.1
  2.2 0.8 %copy-done.1 = f32[7,1024]{1,0:T(8,128)S(1)} copy-done((f32[7,1024]{1,0:T(8,128)S(1)}, f32[7,1024]{1,0:T(8,128)}, u32[]{:S(2)}) %copy-start.1) | copy-done | bytes 28696
  3.0 25.4 %shard_map.68 = (f32[16,8,128]{2,1,0:T(8,128)S(1)}, f32[12,2,3,8,128]{4,3,2,1,0:T(8,128)S(1)}) custom-call(f32[7,1024]{1,0:T(8,128)S(1)} %copy-done.1, s32[1,1024]{1,0:T(1,128)S(1)} %bitcast.4, s32[1,2]{1,0:T(1,128)S(1)} %copy-done.4, f32[36,8,128]{2,1,0:T(8,128)S(1)} %bitcast.3), custom_call_target="tpu_custom_call" | custom-call | tf_op jit(solution)/shard_map/pallas_call | solution.py:214
  28.4 0.0 copy-start.5
  28.4 0.7 copy-done.5
  29.1 21.7 %shard_map.69 = (f32[7,2048]{1,0:T(8,128)}, f32[16,1,128]{2,1,0:T(1,128)S(1)}) custom-call(s32[2,32]{1,0:T(2,128)S(1)} %bitcast.5, s32[1,2]{1,0:T(1,128)S(1)} %copy-done.4, f32[16,8,128]{2,1,0:T(8,128)S(1)} %get-tuple-element.6.sph_ref, f32[12,2,3,8,128]{4,3,2,1,0:T(8,128)S(1)} %get-tuple-element.7.sel_ref), custom_call_target="tpu_custom_call" | custom-call | tf_op jit(solution)/shard_map/pallas_call | solution.py:414
  50.8 0.0 copy-start.2
  50.8 0.6 copy-done.2
  51.4 15.0 %shard_map.70 = f32[1,6]{1,0:T(1,128)} custom-call(f32[16,1,128]{2,1,0:T(1,128)} %copy-done.2), custom_call_target="tpu_custom_call" | custom-call | tf_op jit(solution)/shard_map/pallas_call | solution.py:477
  66.5 1.2 %copy.8 = f32[1,6]{1,0:T(1,128)} copy(f32[1,6]{1,0:T(1,128)} %shard_map.70) | data formatting | bytes 48
Async XLA Ops:
  0.6 0.7 %copy-start.3 = (s32[1024,1]{0,1:T(1,128)S(1)}, s32[1024,1]{0,1:T(1,128)}, u32[]{:S(2)}) copy-start(s32[1024,1]{0,1:T(1,128)} %param.6) | copy-start | bytes 12292
  0.6 0.7 %copy-start.4 = (s32[1,2]{1,0:T(1,128)S(1)}, s32[1,2]{1,0:T(1,128)}, u32[]{:S(2)}) copy-start(s32[1,2]{1,0:T(1,128)} %body_ref.3) | copy-start | bytes 28
  1.3 0.9 %copy-start = (f32[9,1,4096]{2,1,0:T(1,128)S(1)}, f32[9,1,4096]{2,1,0:T(1,128)}, u32[]{:S(2)}) copy-start(f32[9,1,4096]{2,1,0:T(1,128)} %param.9) | copy-start | bytes 442372
  2.2 0.8 %copy-start.1 = (f32[7,1024]{1,0:T(8,128)S(1)}, f32[7,1024]{1,0:T(8,128)}, u32[]{:S(2)}) copy-start(f32[7,1024]{1,0:T(8,128)} %state_ref.1) | copy-start | bytes 86020
  28.4 0.7 %copy-start.5 = (s32[1,2,32]{2,1,0:T(2,128)S(1)}, s32[1,2,32]{2,1,0:T(2,128)}, u32[]{:S(2)}) copy-start(s32[1,2,32]{2,1,0:T(2,128)} %param.8) | copy-start | bytes 772
  50.8 0.6 copy-start.2

commit v2 on v0

v2 whole, which is shorter than its diff:
```python
import functools

import jax
import jax.numpy as jnp
from jax import lax
from jax.experimental import pallas as pl
from jax.experimental.pallas import tpu as pltpu
from jax.sharding import PartitionSpec as P

stiff_pair = 50.0
damp_pair = 2.0
stiff_wall = 50.0
time_step = 0.01
gravity = 9.81
body_mass = 4.0
body_inertia = 40.0

MESH = pl.DeviceIdType.MESH
N = 16
HOLDERS = 12
f32, bf16, i32 = jnp.float32, jnp.bfloat16, jnp.int32


def split3(value):
    high = value.astype(bf16).astype(f32)
    rest = value - high
    middle = rest.astype(bf16).astype(f32)
    return high, middle, rest - middle


def is_holder(s):
    return (s // 4) != (s % 4)


def piece_of(s):
    y, x = s // 4, s % 4
    return 3 * y + x - jnp.where(x > y, 1, 0)


def holder_at(piece):
    y, x = piece // 3, piece % 3
    return 4 * y + x + (1 if x >= y else 0)


def greet(sector, bin_):
    barrier = pltpu.get_barrier_semaphore()
    for off in range(1, N):
        pl.semaphore_signal(barrier, inc=1, device_id=(sector, lax.rem(bin_ + off, N)), device_id_type=MESH)
        pl.semaphore_signal(barrier, inc=1, device_id=(lax.rem(sector + off, N), bin_), device_id_type=MESH)
    return barrier


def outgoing_tiles(state_ref, dest_ref, out_ref):
    leaving = state_ref.shape[1]
    dest = dest_ref[...]
    width = 256
    row = lax.broadcasted_iota(i32, (256, width), 0)
    before = (row < lax.broadcasted_iota(i32, (256, width), 1)).astype(bf16)
    counting = jnp.concatenate([before, jnp.ones((256, width), bf16)], 1)
    carry = jnp.zeros((256, width), f32)
    ranks = []
    for part in range(leaving // width):
        hit = row == dest[:, part * width : (part + 1) * width]
        counted = jnp.dot(hit.astype(bf16), counting, preferred_element_type=f32)
        ranks.append(jnp.sum(jnp.where(hit, counted[:, :width] + carry, 0.0), 0, keepdims=True))
        carry = carry + counted[:, width:]
    rank = jnp.concatenate(ranks, 1).astype(i32)
    key = (dest // N) * 8 + rank
    picks = (lax.broadcasted_iota(i32, (128, leaving), 0) == key).astype(bf16)
    state = state_ref[...]
    state = jnp.concatenate([state, jnp.zeros((1, leaving), f32)], 0)
    stacked = jnp.concatenate(split3(state), 0)
    lane_bin = dest % N
    chosen = [jnp.where(lane_bin == db, stacked, 0.0) for db in range(N)]
    chosen = jnp.concatenate(chosen, 0).astype(bf16)
    placed = lax.dot_general(chosen, picks, (((1,), (1,)), ((), ())), preferred_element_type=f32)
    for db in range(N):
        base = 24 * db
        out_ref[db] = placed[base : base + 8] + placed[base + 8 : base + 16] + placed[base + 16 : base + 24]


def swap_groups(tiles):
    lane = lax.broadcasted_iota(i32, (8, 128), 1)
    for bit in (1, 2, 4, 8):
        low = (lane // 8) % (2 * bit) < bit
        fresh = list(tiles)
        for a in range(N):
            if a & bit == 0:
                b = a | bit
                fresh[a] = jnp.where(low, tiles[a], pltpu.roll(tiles[b], 8 * bit, 1))
                fresh[b] = jnp.where(low, pltpu.roll(tiles[a], 128 - 8 * bit, 1), tiles[b])
        tiles = fresh
    return tiles


def pair_features(sph):
    width = sph.shape[1]
    position, radius = sph[0:3], sph[6:7]
    base = radius * radius - jnp.sum(position * position, 0, keepdims=True)
    base = jnp.where(radius > 0, base, -1e30)
    high, middle, low = split3(jnp.concatenate([position, radius], 0))
    base = jnp.concatenate(split3(base), 0)
    one = jnp.ones((3, width), f32)
    none = jnp.zeros((2, width), f32)
    left = [2.0 * high, 2.0 * high, 2.0 * middle, 2.0 * middle, 2.0 * high, 2.0 * low, base, one, none]
    right = [high, middle, high, middle, low, high, one, base, none]
    row = lax.broadcasted_iota(i32, sph.shape, 0)
    weighed = jnp.where(row == 6, 1.0, sph)
    high, middle, low = split3(weighed)
    stacked = jnp.concatenate([high, middle, low, jnp.zeros_like(high)], 0)
    return (
        jnp.concatenate(left, 0),
        jnp.concatenate(right, 0).astype(bf16),
        stacked.astype(bf16),
    )


def triangle_features(corner):
    a, e1, e2 = corner[0:3], [corner[3 + k] - corner[k] for k in range(3)], [corner[6 + k] - corner[k] for k in range(3)]
    d11 = e1[0] * e1[0] + e1[1] * e1[1] + e1[2] * e1[2]
    d12 = e1[0] * e2[0] + e1[1] * e2[1] + e1[2] * e2[2]
    d22 = e2[0] * e2[0] + e2[1] * e2[1] + e2[2] * e2[2]
    inverse = 1.0 / (d11 * d22 - d12 * d12)
    for_b = [(d22 * e1[k] - d12 * e2[k]) * inverse for k in range(3)]
    for_c = [(d11 * e2[k] - d12 * e1[k]) * inverse for k in range(3)]
    for g in (for_b, for_c):
        g.append(-(g[0] * a[0] + g[1] * a[1] + g[2] * a[2]))
    return [*a, *e1, *e2], [for_b, for_c]


def set_triangles(sel_ref, plain_ref, linear_ref):
    for entry in range(2):
        for group in range(4):
            corner = []
            for c in range(9):
                at = c * 4 + group
                corner.append(sel_ref[at // 3, entry, at % 3])
            plain, (for_b, for_c) = triangle_features(corner)
            for f, value in enumerate(plain):
                plain_ref[entry, pl.ds(8 * group, 8), f, :] = value
            for k, value in enumerate(for_b + for_c):
                linear_ref[entry, pl.ds(8 * group, 8), k, :] = value


def set_spheres(sph_ref, wide_ref, point_ref):
    one, none = jnp.ones((1, 128), f32), jnp.zeros((1, 128), f32)
    for t in range(sph_ref.shape[0]):
        tile = sph_ref[t]
        high, middle, low = split3(tile[0:3])
        high, middle, low = [high, one, high, one], [middle, none, middle, none], [low, none, low, none]
        rows = jnp.concatenate([*high, *high, *middle, *middle, *high, *low], 0)
        point_ref[t] = rows.T.astype(bf16)
        turned = tile.T
        for f, c in enumerate((0, 1, 2, 6)):
            column = turned[:, c : c + 1]
            if c == 6:
                column = column * column
            wide_ref[t, f] = jnp.broadcast_to(column, (128, 128))


def wall_tiles(code_ref, entry, plain_ref, linear_ref, wide_ref, point_ref, coef_refs, push_refs, sums_ref, adds_ref):
    count = code_ref.shape[1]
    lane = lax.broadcasted_iota(i32, (128, 128), 1)
    upper = lax.broadcasted_iota(i32, (8, 128), 0) < 4

    def tiles_of(n):
        code = code_ref[entry, n]
        return code >> 5, code & 31

    def weigh(n, coef_ref):
        st, tt = tiles_of(n)
        high, middle, low = split3(linear_ref[entry, tt])
        rows = [high, middle, high, middle, low, high]
        for_b = jnp.concatenate([jnp.where(upper, g, 0.0) for g in rows], 0)
        for_c = jnp.concatenate([jnp.where(upper, 0.0, g) for g in rows], 0)
        coefficients = jnp.concatenate([for_b, for_c], 1).astype(bf16)
        points = point_ref[st]
        coef_ref[...] = jnp.dot(points, coefficients, preferred_element_type=f32)

    def push(n, coef_ref, push_ref):
        st, tt = tiles_of(n)
        ax, ay, az, ux, uy, uz, wx, wy, wz = (
            jnp.broadcast_to(plain_ref[entry, tt, f : f + 1, :], (8, 128)) for f in range(9)
        )

        def eight(group):
            here = slice(8 * group, 8 * group + 8)
            b, c = coef_ref[here, 0:128], coef_ref[here, 128:256]
            a = jnp.maximum((1.0 - b) - c, 0.0)
            b = jnp.maximum(b, 0.0)
            c = jnp.maximum(c, 0.0)
            total = a + b + c
            inverse = pl.reciprocal(total, approx=True)
            inverse = inverse * (2.0 - total * inverse)
            b, c = b * inverse, c * inverse
            ox = (wide_ref[st, 0, here, :] - ax) - b * ux - c * wx
            oy = (wide_ref[st, 1, here, :] - ay) - b * uy - c * wy
            oz = (wide_ref[st, 2, here, :] - az) - b * uz - c * wz
            strength = jnp.maximum(wide_ref[st, 3, here, :] - (ox * ox + oy * oy + oz * oz), 0.0)
            return strength * ox, strength * oy, strength * oz

        for group in range(8):
            here = slice(16 * group, 16 * group + 16)
            for k, both in enumerate(zip(eight(2 * group), eight(2 * group + 1))):
                value = jnp.concatenate(both, 0)
                high = value.astype(bf16)
                push_ref[here, 128 * k : 128 * k + 128] = high
                push_ref[here, 384 + 128 * k : 512 + 128 * k] = (value - high.astype(f32)).astype(bf16)

    def add_up(n, push_ref):
        added = jnp.dot(push_ref[...], adds_ref[...], preferred_element_type=f32)
        sums_ref[entry] = jnp.where((lane & 31) == n, added, sums_ref[entry])

    weigh(0, coef_refs[0])
    push_refs[1][...] = jnp.zeros_like(push_refs[1])

    def two_tiles(i, carry):
        n = 2 * i
        weigh(n + 1, coef_refs[1])
        push(n, coef_refs[0], push_refs[0])
        add_up(n - 1, push_refs[1])
        weigh(jnp.minimum(n + 2, count - 1), coef_refs[0])
        push(n + 1, coef_refs[1], push_refs[1])
        add_up(n, push_refs[0])
        return carry

    lax.fori_loop(0, count // 2, two_tiles, 0)
    add_up(count - 1, push_refs[1])


def set_adds(adds_ref):
    block = lax.broadcasted_iota(i32, (6 * 128, 128), 0) >> 7
    block = jnp.where(block < 3, block, block - 3)
    adds_ref[...] = (block == (lax.broadcasted_iota(i32, (6 * 128, 128), 1) >> 5)).astype(bf16)


def set_pairs(sph_ref, left_ref, right_ref, stacked_ref, summed_ref):
    for t in range(sph_ref.shape[0]):
        left, right, stacked = pair_features(sph_ref[t])
        lanes = slice(128 * t, 128 * t + 128)
        left_ref[pl.ds(128 * t, 128), :] = left.T.astype(bf16)
        right_ref[:, lanes], stacked_ref[:, lanes] = right, stacked
    summed_ref[...] = jnp.zeros_like(summed_ref)


def pair_sums(first, last, left_ref, right_ref, stacked_ref, summed_ref):
    rows = 256

    def row_group(step, carry):
        start = pl.multiple_of(step * rows, rows)
        left = left_ref[pl.ds(start, rows), :]
        weighed = stacked_ref[:, pl.ds(start, rows)]
        for column in range(0, right_ref.shape[1], 256):
            here = slice(column, column + 256)
            gap = jnp.dot(left, right_ref[:, here], preferred_element_type=f32)
            inter = jnp.maximum(gap, 0.0)
            high = inter.astype(bf16)
            low = (inter - high.astype(f32)).astype(bf16)
            summed_ref[:, here] += jnp.dot(weighed, high, preferred_element_type=f32) + jnp.dot(
                weighed, low, preferred_element_type=f32
            )
        return carry

    lax.fori_loop(first, last, row_group, 0)


def wall_forces(codes, entry, sums_ref):
    turned = sums_ref[entry].T
    tiles = lax.broadcasted_iota(i32, (16, codes.shape[1]), 0)
    chosen = (tiles == codes >> 5).astype(f32)
    return [
        stiff_wall * jnp.dot(chosen, turned[32 * k : 32 * k + 32], precision=lax.Precision.HIGHEST, preferred_element_type=f32)
        for k in range(3)
    ]


def wrench_line(sph_ref, force):
    tiles = sph_ref.shape[0]
    pos = [jnp.concatenate([sph_ref[t, k : k + 1, :] for t in range(tiles)], 0) for k in range(3)]
    moment = [
        pos[1] * force[2] - pos[2] * force[1],
        pos[2] * force[0] - pos[0] * force[2],
        pos[0] * force[1] - pos[1] * force[0],
    ]
    lane = lax.broadcasted_iota(i32, (1, 128), 1)
    line = jnp.zeros((1, 128), f32)
    for k, value in enumerate(force + moment):
        line = jnp.where(lane == k, -jnp.sum(jnp.sum(value, 0, keepdims=True), 1, keepdims=True), line)
    return line


def set_state(sph_ref, summed_ref, wall, state_out):
    falling = jnp.where(lax.broadcasted_iota(i32, (3, 128), 0) == 2, gravity, 0.0)
    for t in range(sph_ref.shape[0]):
        lanes = slice(128 * t, 128 * t + 128)
        tile = sph_ref[t]
        pos, vel, radius = tile[0:3], tile[3:6], tile[6:7]
        weighted = summed_ref[0:8, lanes] + summed_ref[8:16, lanes] + summed_ref[16:24, lanes]
        totals = weighted[6:7]
        live = radius > 0
        mass = jnp.where(live, radius * radius * radius, 1.0)
        pair = stiff_pair * (totals * pos - weighted[0:3]) - damp_pair * (totals * vel - weighted[3:6])
        push = jnp.concatenate([wall[k][t : t + 1] for k in range(3)], 0)
        fresh = vel + time_step * ((pair + push) / mass - falling)
        block = jnp.concatenate([pos + time_step * fresh, fresh, radius], 0)
        state_out[:, lanes] = jnp.where(live, block, 0.0)


def step_kernel(
    state_ref, dest_ref, body_ref, code_ref, codes_ref, tri_ref, state_out, kick_out,
    out1, got1, out2, sph, piece, sel_send, sel, names, names_got, names_smem,
    wide, point, plain, linear, coef0, coef1, push0, push1, sums, adds, left, right, stacked, summed,
    part, part_got, row, row_got,
    s1, r1, s2, r2, t1s, t1r, ns, nr, t2s, t2r, w1s, w1r, w2s, w2r, own_sem, names_sem,
):
    sector, bin_ = lax.axis_index("sector"), lax.axis_index("bin")
    barrier = greet(sector, bin_)
    outgoing_tiles(state_ref, dest_ref, out1)
    lane = lax.broadcasted_iota(i32, (1, 128), 1)
    names[...] = jnp.where(lane == 0, body_ref[0, 0], body_ref[0, 1])
    set_adds(adds)
    pl.semaphore_wait(barrier, 2 * (N - 1))

    def along_sector(source, landing, sent, arrived):
        def copy(src, dst):
            return pltpu.make_async_remote_copy(
                src_ref=source(dst), dst_ref=landing(src), send_sem=sent.at[dst], recv_sem=arrived.at[src],
                device_id=(dst, bin_), device_id_type=MESH,
            )

        return copy

    def along_bin(source, landing, sent, arrived):
        def copy(src, dst):
            return pltpu.make_async_remote_copy(
                src_ref=source(dst), dst_ref=landing(src), send_sem=sent.at[dst], recv_sem=arrived.at[src],
                device_id=(sector, dst), device_id_type=MESH,
            )

        return copy

    def peers(me):
        return [lax.rem(me + off, N) for off in range(1, N)]

    sphere_one = along_bin(lambda d: out1.at[d], lambda s: got1.at[s], s1, r1)
    sphere_two = along_sector(lambda d: out2.at[d], lambda s: sph.at[s], s2, r2)
    piece_one = along_sector(lambda d: tri_ref.at[pl.ds(3 * piece_of(d), 3)], lambda s: piece.at[s], t1s, t1r)
    names_one = along_sector(lambda d: names, lambda s: names_got.at[s], ns, nr)
    piece_two = along_sector(lambda d: sel_send.at[d], lambda s: sel.at[piece_of(s)], t2s, t2r)
    wrench_one = along_sector(lambda d: part.at[d], lambda s: part_got.at[s], w1s, w1r)
    wrench_two = along_bin(lambda d: row, lambda s: row_got.at[s], w2s, w2r)

    holding = is_holder(sector)
    for peer in peers(bin_):
        sphere_one(bin_, peer).start()
    for peer in peers(sector):

        @pl.when(is_holder(peer))
        def _(peer=peer):
            names_one(sector, peer).start()
            piece_one(sector, peer).start()

    @pl.when(holding)
    def _():
        own = pltpu.make_async_copy(tri_ref.at[pl.ds(3 * piece_of(sector), 3)], piece.at[sector], own_sem)
        own.start()
        names_got[sector] = names[...]
        own.wait()

    got1[bin_] = out1[bin_]
    for peer in peers(bin_):
        sphere_one(peer, bin_).wait_recv()
    for ds, tile in enumerate(swap_groups([got1[sb] for sb in range(N)])):
        out2[ds] = tile
    for peer in peers(sector):
        sphere_two(sector, peer).start()
    sph[sector] = out2[sector]

    @pl.when(holding)
    def _():
        for peer in peers(sector):
            names_one(peer, sector).wait_recv()
        listed = pltpu.make_async_copy(names_got, names_smem, names_sem)
        listed.start()
        for peer in peers(sector):
            piece_one(peer, sector).wait_recv()
        listed.wait()
        for dst in range(N):
            for entry in range(2):
                sel_send[dst, entry] = piece[names_smem[dst, 0, entry]]
        for peer in peers(sector):
            piece_two(sector, peer).start()
        sel[piece_of(sector)] = sel_send[sector]

    for peer in peers(sector):
        sphere_two(peer, sector).wait_recv()
    set_spheres(sph, wide, point)
    set_pairs(sph, left, right, stacked, summed)
    pair_sums(0, PAIRS_ONE, left, right, stacked, summed)

    for peer in peers(sector):

        @pl.when(is_holder(peer))
        def _(peer=peer):
            piece_two(peer, sector).wait_recv()

    set_triangles(sel, plain, linear)
    body_row = lax.broadcasted_iota(i32, (N, 1, 128), 0)
    parts = jnp.zeros((N, 1, 128), f32)
    wall = [jnp.zeros((16, 128), f32)] * 3
    for entry in range(2):
        sums[entry] = jnp.zeros((128, 128), f32)
        wall_tiles(code_ref, entry, plain, linear, wide, point, (coef0, coef1), (push0, push1), sums, adds)
        force = wall_forces(codes_ref[entry : entry + 1, :], entry, sums)
        wall = [w + g for w, g in zip(wall, force)]
        parts = parts + jnp.where(body_row == body_ref[0, entry], wrench_line(sph, force)[None], 0.0)
    part[...] = parts

    for peer in peers(sector):
        wrench_one(sector, peer).start()
    part_got[sector] = part[sector]
    pair_sums(PAIRS_ONE, PAIRS_TWO, left, right, stacked, summed)
    for peer in peers(sector):
        wrench_one(peer, sector).wait_recv()
    row[...] = functools.reduce(jnp.add, [part_got[k] for k in range(N)])
    for peer in peers(bin_):
        wrench_two(bin_, peer).start()
    row_got[bin_] = row[...]
    pair_sums(PAIRS_TWO, PAIRS_ALL, left, right, stacked, summed)
    set_state(sph, summed, wall, state_out)
    for peer in peers(bin_):
        wrench_two(peer, bin_).wait_recv()
    total = functools.reduce(jnp.add, [row_got[k] for k in range(N)])
    total = total * jnp.where(lane < 3, time_step / body_mass, time_step / body_inertia)
    kick_out[...] = total[:, 0:6]

    for peer in peers(bin_):
        sphere_one(bin_, peer).wait_send()
        wrench_two(bin_, peer).wait_send()
    for peer in peers(sector):
        sphere_two(sector, peer).wait_send()
        wrench_one(sector, peer).wait_send()

        @pl.when(is_holder(peer))
        def _(peer=peer):
            names_one(sector, peer).wait_send()
            piece_one(sector, peer).wait_send()

    @pl.when(holding)
    def _():
        for peer in peers(sector):
            piece_two(sector, peer).wait_send()


PAIRS_ONE, PAIRS_TWO, PAIRS_ALL = 3, 6, 8


def step(state, dest, bodies, codes, tri):
    slots = 2 * state.shape[1]
    smem, vmem = pl.BlockSpec(memory_space=pltpu.SMEM), pl.BlockSpec(memory_space=pltpu.VMEM)
    dma = pltpu.SemaphoreType.DMA
    line = pltpu.VMEM((N, 1, 128), f32)
    tiles = pltpu.VMEM((N, 8, 128), f32)
    return pl.pallas_call(
        step_kernel,
        out_shape=(jax.ShapeDtypeStruct((7, slots), f32), jax.ShapeDtypeStruct((1, 6), f32)),
        in_specs=[vmem, vmem, smem, smem, vmem, pl.BlockSpec(memory_space=pl.ANY)],
        out_specs=(vmem, vmem),
        scratch_shapes=[
            *[tiles] * 4,
            pltpu.VMEM((N, 3, 8, 128), f32),
            pltpu.VMEM((N, 2, 3, 8, 128), f32),
            pltpu.VMEM((HOLDERS, 2, 3, 8, 128), f32),
            pltpu.VMEM((1, 128), i32),
            pltpu.VMEM((N, 1, 128), i32),
            pltpu.SMEM((N, 1, 128), i32),
            pltpu.VMEM((N, 4, 128, 128), f32),
            pltpu.VMEM((N, 128, 48), bf16),
            pltpu.VMEM((2, 32, 16, 128), f32),
            pltpu.VMEM((2, 32, 8, 128), f32),
            pltpu.VMEM((128, 256), f32),
            pltpu.VMEM((128, 256), f32),
            pltpu.VMEM((128, 768), bf16),
            pltpu.VMEM((128, 768), bf16),
            pltpu.VMEM((2, 128, 128), f32),
            pltpu.VMEM((768, 128), bf16),
            pltpu.VMEM((slots, 32), bf16),
            pltpu.VMEM((32, slots), bf16),
            pltpu.VMEM((32, slots), bf16),
            pltpu.VMEM((32, slots), f32),
            line,
            line,
            pltpu.VMEM((1, 128), f32),
            line,
        ]
        + [dma((N,))] * 14
        + [dma, dma],
        compiler_params=pltpu.CompilerParams(collective_id=0, has_side_effects=True, vmem_limit_bytes=40 * 2**20),
    )(state, dest, bodies, codes, codes, tri)


def local(sph_state, sph_dest, body_list, tile_codes, triangles):
    dest = sph_dest.reshape(1, -1)
    tri = triangles.reshape(36, 8, 128)
    return step(sph_state, dest, body_list, tile_codes[0], tri)


def solution(mesh):
    return jax.shard_map(
        local,
        mesh=mesh,
        in_specs=(
            P(None, ("sector", "bin")),
            P(("sector", "bin"), None),
            P(("sector", "bin"), None),
            P(("sector", "bin"), None, None),
            P(None, "sector", "bin"),
        ),
        out_specs=(P(None, ("sector", "bin")), P("sector", None)),
        check_vma=False,
    )
```

time: 451 us -> 56.7 us (0.13)
  loops' own time: 180 us -> 0 us
  other arithmetic: 71.6 us -> 0 us
  blocking collectives: 63.7 us -> 0 us
  local copies, waits for them, and re-layouts: 56 us -> 3.48 us
  Pallas kernels: 0 us -> 52.3 us
  matrix products: 32.3 us -> 0 us
  starting transfers between devices: 17.6 us -> 0 us
  between operations: 18.1 us -> 0.67 us
  waiting for transfers between devices: 7.67 us -> 0 us
    another operation x3 -> x0, loops' own time: 180 us -> none  [the longest x2 172 us: tile_forces(): (forces, wrench), unused = lax.scan(advance_tile, initial, tile_list)]
    pallas_call x0 -> x1, Pallas kernels: none -> 52.3 us  [step(): pl.pallas_call(step_kernel, out_shape=(jax.ShapeDtypeStruct((7, slots), f...]
    reduce_sum x322 -> x0, other arithmetic: 49.3 us -> none  [the longest x64 19.1 us: contact(): on_body = -jnp.sum(forces, (1, 2))]
    dynamic_slice x140 -> x0, local copies, waits for them, and re-layouts: 40.9 us -> none  [the longest x64 37.3 us: tile_forces(): (forces, wrench), unused = lax.scan(advance_tile, initial, tile_list)]
    unnamed x1 -> x0, blocking collectives: 33.5 us -> none
    dot_general x8 -> x0, matrix products: 32.3 us -> none  [the longest x4 17.9 us: row_group(): lax.dot_general(stacked, intersection, (((1,), (1,)), ((), ())), precisio...]
    psum x1 -> x0, blocking collectives: 30.3 us -> none  [bin_total(): return lax.psum(partial_row, 'bin')]
    all_to_all x2 -> x0, starting transfers between devices: 17.6 us -> none  [the longest x1 9.99 us: local(): lax.all_to_all(lax.all_to_all(outgoing, 'sector', split_axis=1, concat_ax...]
  transfers between devices with their start and end apart: 3 -> 0, of which waited for: 1 -> 0; matrix products, arithmetic and copies ran while one was open for 10% -> 0% of each run, Pallas kernels for 0% -> 0%
where the time goes in v2:
time: 56.7 us; the launch traced here: 56.5 us
  Pallas kernels  52.3 us (92%)
  local copies, waits for them, and re-layouts  3.48 us (6%)
  between operations  0.67 us (1%)
    pallas_call x1, Pallas kernels, step(): pl.pallas_call(step_kernel, out_shape=(jax.ShapeDtypeStruct((7, slots), f...  52.3 us
    unnamed x12, local copies, waits for them, and re-layouts  3.48 us

profile of v2, /device:TPU:1, one launch (start us, length us, event | category | flops | bytes accessed | tf_op | source)
XLA Modules:
  0.0 56.5 jit_solution(5247083961026430610)
XLA Ops:
  0.6 0.0 copy-start.3
  0.6 0.0 copy-start.2
  0.7 0.0 copy-start.4
  0.7 0.7 %copy-done.3 = s32[1024,1]{0,1:T(1,128)S(1)} copy-done((s32[1024,1]{0,1:T(1,128)S(1)}, s32[1024,1]{0,1:T(1,128)}, u32[]{:S(2)}) %copy-start.3) | copy-done | bytes 4120
  1.3 0.0 copy-done.2
  1.3 0.0 copy-done.4
  1.3 0.0 copy-start
  1.3 0.9 %copy-done = f32[9,1,4096]{2,1,0:T(1,128)S(1)} copy-done((f32[9,1,4096]{2,1,0:T(1,128)S(1)}, f32[9,1,4096]{2,1,0:T(1,128)}, u32[]{:S(2)}) %copy-start) | copy-done | bytes 147480
  2.2 0.0 copy-start.1
  2.2 0.8 %copy-done.1 = f32[7,1024]{1,0:T(8,128)S(1)} copy-done((f32[7,1024]{1,0:T(8,128)S(1)}, f32[7,1024]{1,0:T(8,128)}, u32[]{:S(2)}) %copy-start.1) | copy-done | bytes 28696
  3.0 52.3 %shard_map.68 = (f32[7,2048]{1,0:T(8,128)S(1)}, f32[1,6]{1,0:T(1,128)S(1)}) custom-call(f32[7,1024]{1,0:T(8,128)S(1)} %copy-done.1, s32[1,1024]{1,0:T(1,128)S(1)} %bitcast.6, s32[1,2]{1,0:T(1,128)S(1)} %copy-done.4, s32[2,32]{1,0:T(2,128)S(1)} %bitcast.4, s32[2,32]{1,0:T(2,128)S(1)} %bitcast.5, f32[36,8,128]{2,1,0:T(8,128)S(1)} %bitcast.3), custom_call_target="tpu_custom_call" | custom-call | tf_op jit(solution)/shard_map/pallas_call | solution.py:464
  55.3 0.6 %copy.9 = f32[7,2048]{1,0:T(8,128)} copy(f32[7,2048]{1,0:T(8,128)S(1)} %get-tuple-element.4) | data formatting | bytes 114688
  55.9 0.5 copy.10
Async XLA Ops:
  0.6 0.7 %copy-start.3 = (s32[1024,1]{0,1:T(1,128)S(1)}, s32[1024,1]{0,1:T(1,128)}, u32[]{:S(2)}) copy-start(s32[1024,1]{0,1:T(1,128)} %param.6) | copy-start | bytes 12292
  0.6 0.7 %copy-start.2 = (s32[1,2,32]{2,1,0:T(2,128)S(1)}, s32[1,2,32]{2,1,0:T(2,128)}, u32[]{:S(2)}) copy-start(s32[1,2,32]{2,1,0:T(2,128)} %param.8) | copy-start | bytes 772
  0.7 0.7 %copy-start.4 = (s32[1,2]{1,0:T(1,128)S(1)}, s32[1,2]{1,0:T(1,128)}, u32[]{:S(2)}) copy-start(s32[1,2]{1,0:T(1,128)} %body_ref.1) | copy-start | bytes 28
  1.3 0.9 %copy-start = (f32[9,1,4096]{2,1,0:T(1,128)S(1)}, f32[9,1,4096]{2,1,0:T(1,128)}, u32[]{:S(2)}) copy-start(f32[9,1,4096]{2,1,0:T(1,128)} %param.9) | copy-start | bytes 442372
  2.2 0.8 %copy-start.1 = (f32[7,1024]{1,0:T(8,128)S(1)}, f32[7,1024]{1,0:T(8,128)}, u32[]{:S(2)}) copy-start(f32[7,1024]{1,0:T(8,128)} %state_ref.1) | copy-start | bytes 86020

commit v3 on v2

--- a/solution.py
+++ b/solution.py
@@ -307,14 +307,30 @@
 
 
 def step_kernel(
-    state_ref, dest_ref, body_ref, code_ref, codes_ref, tri_ref, state_out, kick_out,
+    state_hbm, dest_hbm, body_hbm, code_hbm, tri_ref, state_out, kick_out,
+    state_ref, dest_ref, body_ref, code_ref, codes_ref,
     out1, got1, out2, sph, piece, sel_send, sel, names, names_got, names_smem,
     wide, point, plain, linear, coef0, coef1, push0, push1, sums, adds, left, right, stacked, summed,
     part, part_got, row, row_got,
     s1, r1, s2, r2, t1s, t1r, ns, nr, t2s, t2r, w1s, w1r, w2s, w2r, own_sem, names_sem,
+    in0, in1, in2, in3, in4,
 ):
     sector, bin_ = lax.axis_index("sector"), lax.axis_index("bin")
+    inputs = [
+        pltpu.make_async_copy(source, target, semaphore)
+        for source, target, semaphore in (
+            (dest_hbm, dest_ref, in0),
+            (state_hbm, state_ref, in1),
+            (body_hbm, body_ref, in2),
+            (code_hbm, code_ref, in3),
+            (code_hbm, codes_ref, in4),
+        )
+    ]
+    for copy in inputs:
+        copy.start()
     barrier = greet(sector, bin_)
+    for copy in inputs:
+        copy.wait()
     outgoing_tiles(state_ref, dest_ref, out1)
     lane = lax.broadcasted_iota(i32, (1, 128), 1)
     names[...] = jnp.where(lane == 0, body_ref[0, 0], body_ref[0, 1])
@@ -324,7 +340,7 @@
     def along_sector(source, landing, sent, arrived):
         def copy(src, dst):
             return pltpu.make_async_remote_copy(
-                src_ref=source(dst), dst_ref=landing(src), send_sem=sent.at[dst], recv_sem=arrived.at[src],
+                src_ref=source(dst), dst_ref=landing(src), send_sem=sent, recv_sem=arrived,
                 device_id=(dst, bin_), device_id_type=MESH,
             )
 
@@ -333,7 +349,7 @@
     def along_bin(source, landing, sent, arrived):
         def copy(src, dst):
             return pltpu.make_async_remote_copy(
-                src_ref=source(dst), dst_ref=landing(src), send_sem=sent.at[dst], recv_sem=arrived.at[src],
+                src_ref=source(dst), dst_ref=landing(src), send_sem=sent, recv_sem=arrived,
                 device_id=(sector, dst), device_id_type=MESH,
             )
 
@@ -341,6 +357,10 @@
 
     def peers(me):
         return [lax.rem(me + off, N) for off in range(1, N)]
+
+    def all_of(buffer, count, semaphore):
+        view = buffer.at[pl.ds(0, count)]
+        pltpu.make_async_copy(view, view, semaphore).wait()
 
     sphere_one = along_bin(lambda d: out1.at[d], lambda s: got1.at[s], s1, r1)
     sphere_two = along_sector(lambda d: out2.at[d], lambda s: sph.at[s], s2, r2)
@@ -368,8 +388,7 @@
         own.wait()
 
     got1[bin_] = out1[bin_]
-    for peer in peers(bin_):
-        sphere_one(peer, bin_).wait_recv()
+    all_of(got1, N - 1, r1)
     for ds, tile in enumerate(swap_groups([got1[sb] for sb in range(N)])):
         out2[ds] = tile
     for peer in peers(sector):
@@ -378,12 +397,10 @@
 
     @pl.when(holding)
     def _():
-        for peer in peers(sector):
-            names_one(peer, sector).wait_recv()
+        all_of(names_got, N - 1, nr)
         listed = pltpu.make_async_copy(names_got, names_smem, names_sem)
         listed.start()
-        for peer in peers(sector):
-            piece_one(peer, sector).wait_recv()
+        all_of(piece, N - 1, t1r)
         listed.wait()
         for dst in range(N):
             for entry in range(2):
@@ -392,17 +409,18 @@
             piece_two(sector, peer).start()
         sel[piece_of(sector)] = sel_send[sector]
 
-    for peer in peers(sector):
-        sphere_two(peer, sector).wait_recv()
+    all_of(sph, N - 1, r2)
     set_spheres(sph, wide, point)
     set_pairs(sph, left, right, stacked, summed)
     pair_sums(0, PAIRS_ONE, left, right, stacked, summed)
 
-    for peer in peers(sector):
-
-        @pl.when(is_holder(peer))
-        def _(peer=peer):
-            piece_two(peer, sector).wait_recv()
+    @pl.when(holding)
+    def _():
+        all_of(sel, HOLDERS - 1, t2r)
+
+    @pl.when(jnp.logical_not(holding))
+    def _():
+        all_of(sel, HOLDERS, t2r)
 
     set_triangles(sel, plain, linear)
     body_row = lax.broadcasted_iota(i32, (N, 1, 128), 0)
@@ -420,36 +438,33 @@
         wrench_one(sector, peer).start()
     part_got[sector] = part[sector]
     pair_sums(PAIRS_ONE, PAIRS_TWO, left, right, stacked, summed)
-    for peer in peers(sector):
-        wrench_one(peer, sector).wait_recv()
+    all_of(part_got, N - 1, w1r)
     row[...] = functools.reduce(jnp.add, [part_got[k] for k in range(N)])
     for peer in peers(bin_):
         wrench_two(bin_, peer).start()
     row_got[bin_] = row[...]
     pair_sums(PAIRS_TWO, PAIRS_ALL, left, right, stacked, summed)
     set_state(sph, summed, wall, state_out)
-    for peer in peers(bin_):
-        wrench_two(peer, bin_).wait_recv()
+    all_of(row_got, N - 1, w2r)
     total = functools.reduce(jnp.add, [row_got[k] for k in range(N)])
     total = total * jnp.where(lane < 3, time_step / body_mass, time_step / body_inertia)
     kick_out[...] = total[:, 0:6]
 
-    for peer in peers(bin_):
-        sphere_one(bin_, peer).wait_send()
-        wrench_two(bin_, peer).wait_send()
-    for peer in peers(sector):
-        sphere_two(sector, peer).wait_send()
-        wrench_one(sector, peer).wait_send()
-
-        @pl.when(is_holder(peer))
-        def _(peer=peer):
-            names_one(sector, peer).wait_send()
-            piece_one(sector, peer).wait_send()
+    all_of(out1, N - 1, s1)
+    all_of(out2, N - 1, s2)
+    all_of(part, N - 1, w1s)
+    all_of(row_got, N - 1, w2s)
 
     @pl.when(holding)
     def _():
-        for peer in peers(sector):
-            piece_two(sector, peer).wait_send()
+        all_of(names_got, HOLDERS - 1, ns)
+        all_of(piece, HOLDERS - 1, t1s)
+        all_of(sel_send, N - 1, t2s)
+
+    @pl.when(jnp.logical_not(holding))
+    def _():
+        all_of(names_got, HOLDERS, ns)
+        all_of(piece, HOLDERS, t1s)
 
 
 PAIRS_ONE, PAIRS_TWO, PAIRS_ALL = 3, 6, 8
@@ -457,16 +472,21 @@
 
 def step(state, dest, bodies, codes, tri):
     slots = 2 * state.shape[1]
-    smem, vmem = pl.BlockSpec(memory_space=pltpu.SMEM), pl.BlockSpec(memory_space=pltpu.VMEM)
+    vmem = pl.BlockSpec(memory_space=pltpu.VMEM)
     dma = pltpu.SemaphoreType.DMA
     line = pltpu.VMEM((N, 1, 128), f32)
     tiles = pltpu.VMEM((N, 8, 128), f32)
     return pl.pallas_call(
         step_kernel,
         out_shape=(jax.ShapeDtypeStruct((7, slots), f32), jax.ShapeDtypeStruct((1, 6), f32)),
-        in_specs=[vmem, vmem, smem, smem, vmem, pl.BlockSpec(memory_space=pl.ANY)],
+        in_specs=[pl.BlockSpec(memory_space=pltpu.HBM)] * 5,
         out_specs=(vmem, vmem),
         scratch_shapes=[
+            pltpu.VMEM(state.shape, f32),
+            pltpu.VMEM(dest.shape, i32),
+            pltpu.SMEM(bodies.shape, i32),
+            pltpu.SMEM(codes.shape, i32),
+            pltpu.VMEM(codes.shape, i32),
             *[tiles] * 4,
             pltpu.VMEM((N, 3, 8, 128), f32),
             pltpu.VMEM((N, 2, 3, 8, 128), f32),
@@ -493,10 +513,9 @@
             pltpu.VMEM((1, 128), f32),
             line,
         ]
-        + [dma((N,))] * 14
-        + [dma, dma],
-        compiler_params=pltpu.CompilerParams(collective_id=0, has_side_effects=True, vmem_limit_bytes=40 * 2**20),
-    )(state, dest, bodies, codes, codes, tri)
+        + [dma] * 21,
+        compiler_params=pltpu.CompilerParams(collective_id=0, has_side_effects=True, vmem_limit_bytes=60 * 2**20),
+    )(state, dest, bodies, codes, tri)
 
 
 def local(sph_state, sph_dest, body_list, tile_codes, triangles):

time: 56.7 us -> 53 us (0.935)
  Pallas kernels: 52.3 us -> 50.1 us
  local copies, waits for them, and re-layouts: 3.48 us -> 1.99 us
    pallas_call x1, Pallas kernels: 52.3 us -> 50.1 us  [step(): pl.pallas_call(step_kernel, out_shape=(jax.ShapeDtypeStruct((7, slots), f...]
    unnamed x12 -> x4, local copies, waits for them, and re-layouts: 3.48 us -> 1.99 us
where the time goes in v3:
time: 53 us; the launch traced here: 52.8 us
  Pallas kernels  50.1 us (95%)
  local copies, waits for them, and re-layouts  1.99 us (4%)
  between operations  0.65 us (1%)
    pallas_call x1, Pallas kernels, step(): pl.pallas_call(step_kernel, out_shape=(jax.ShapeDtypeStruct((7, slots), f...  50.1 us
    unnamed x4, local copies, waits for them, and re-layouts  1.99 us

profile of v3, /device:TPU:1, one launch (start us, length us, event | category | flops | bytes accessed | tf_op | source)
XLA Modules:
  0.0 52.8 jit_solution(8989491354319047066)
XLA Ops:
  0.6 50.1 %shard_map.68 = (f32[7,2048]{1,0:T(8,128)}, f32[1,6]{1,0:T(1,128)}) custom-call(f32[7,1024]{1,0:T(8,128)} %state_hbm.1, s32[1,1024]{1,0:T(1,128)} %bitcast.4, s32[1,2]{1,0:T(1,128)} %body_hbm.1, s32[2,32]{1,0:T(2,128)} %bitcast.5, f32[36,8,128]{2,1,0:T(8,128)} %bitcast.3), custom_call_target="tpu_custom_call" | custom-call | tf_op jit(solution)/shard_map/pallas_call | solution.py:479
  50.8 0.0 copy-start
  50.8 1.5 %copy.9 = f32[7,2048]{1,0:T(8,128)} copy(f32[7,2048]{1,0:T(8,128)} %get-tuple-element.4) | data formatting | bytes 114688
  52.3 0.0 copy-done
  52.3 0.5 copy.10
Async XLA Ops:
  50.8 1.5 %copy-start = (f32[1,6]{1,0:T(1,128)S(1)}, f32[1,6]{1,0:T(1,128)}, u32[]{:S(2)}) copy-start(f32[1,6]{1,0:T(1,128)} %get-tuple-element.5) | copy-start | bytes 76

commit v4 on v3

--- a/solution.py
+++ b/solution.py
@@ -158,9 +158,8 @@
             wide_ref[t, f] = jnp.broadcast_to(column, (128, 128))
 
 
-def wall_tiles(code_ref, entry, plain_ref, linear_ref, wide_ref, point_ref, coef_refs, push_refs, sums_ref, adds_ref):
+def wall_tiles(code_ref, entry, plain_ref, linear_ref, wide_ref, point_ref, coef_refs, slot_ref, order_ref):
     count = code_ref.shape[1]
-    lane = lax.broadcasted_iota(i32, (128, 128), 1)
     upper = lax.broadcasted_iota(i32, (8, 128), 0) < 4
 
     def tiles_of(n):
@@ -177,8 +176,9 @@
         points = point_ref[st]
         coef_ref[...] = jnp.dot(points, coefficients, preferred_element_type=f32)
 
-    def push(n, coef_ref, push_ref):
+    def push(n, coef_ref):
         st, tt = tiles_of(n)
+        before = order_ref[entry, n]
         ax, ay, az, ux, uy, uz, wx, wy, wz = (
             jnp.broadcast_to(plain_ref[entry, tt, f : f + 1, :], (8, 128)) for f in range(9)
         )
@@ -199,33 +199,49 @@
             strength = jnp.maximum(wide_ref[st, 3, here, :] - (ox * ox + oy * oy + oz * oz), 0.0)
             return strength * ox, strength * oy, strength * oz
 
-        for group in range(8):
-            here = slice(16 * group, 16 * group + 16)
-            for k, both in enumerate(zip(eight(2 * group), eight(2 * group + 1))):
-                value = jnp.concatenate(both, 0)
-                high = value.astype(bf16)
-                push_ref[here, 128 * k : 128 * k + 128] = high
-                push_ref[here, 384 + 128 * k : 512 + 128 * k] = (value - high.astype(f32)).astype(bf16)
-
-    def add_up(n, push_ref):
-        added = jnp.dot(push_ref[...], adds_ref[...], preferred_element_type=f32)
-        sums_ref[entry] = jnp.where((lane & 31) == n, added, sums_ref[entry])
+        def held(first):
+            return [[slot_ref[entry, before, k, 8 * g : 8 * g + 8, :] for k in range(3)] for g in range(first, first + 2)]
+
+        for first in range(0, 16, 2):
+            earlier = held(first)
+            for g in range(2):
+                here = slice(8 * (first + g), 8 * (first + g) + 8)
+                for k, value in enumerate(eight(first + g)):
+                    slot_ref[entry, n, k, here, :] = earlier[g][k] + value
 
     weigh(0, coef_refs[0])
-    push_refs[1][...] = jnp.zeros_like(push_refs[1])
 
     def two_tiles(i, carry):
         n = 2 * i
         weigh(n + 1, coef_refs[1])
-        push(n, coef_refs[0], push_refs[0])
-        add_up(n - 1, push_refs[1])
+        push(n, coef_refs[0])
         weigh(jnp.minimum(n + 2, count - 1), coef_refs[0])
-        push(n + 1, coef_refs[1], push_refs[1])
-        add_up(n, push_refs[0])
+        push(n + 1, coef_refs[1])
         return carry
 
     lax.fori_loop(0, count // 2, two_tiles, 0)
-    add_up(count - 1, push_refs[1])
+
+
+def set_order(code_ref, order_ref):
+    count = code_ref.shape[1]
+    row = lax.broadcasted_iota(i32, (count, 128), 0)
+    lane = lax.broadcasted_iota(i32, (count, 128), 1)
+
+    def latest(hit):
+        found = jnp.where(hit, row, -1)
+        found = functools.reduce(jnp.maximum, [found[8 * g : 8 * g + 8] for g in range(count // 8)])
+        for shift in (4, 2, 1):
+            found = jnp.maximum(found, pltpu.roll(found, shift, 0))
+        return jnp.where(found < 0, count, found)[0:1]
+
+    for entry in range(2):
+        down, along = jnp.zeros((count, 128), i32), jnp.full((count, 128), -1, i32)
+        for n in range(count):
+            tile = code_ref[entry, n] >> 5
+            down = jnp.where(row == n, tile, down)
+            along = jnp.where(lane == n, tile, along)
+        order_ref[entry : entry + 1, :] = latest((down == along) & (row < lane))
+        order_ref[2 + entry : 3 + entry, :] = latest(down == lane)
 
 
 def set_adds(adds_ref):
@@ -264,28 +280,46 @@
     lax.fori_loop(first, last, row_group, 0)
 
 
-def wall_forces(codes, entry, sums_ref):
-    turned = sums_ref[entry].T
-    tiles = lax.broadcasted_iota(i32, (16, codes.shape[1]), 0)
-    chosen = (tiles == codes >> 5).astype(f32)
-    return [
-        stiff_wall * jnp.dot(chosen, turned[32 * k : 32 * k + 32], precision=lax.Precision.HIGHEST, preferred_element_type=f32)
-        for k in range(3)
-    ]
-
-
-def wrench_line(sph_ref, force):
-    tiles = sph_ref.shape[0]
-    pos = [jnp.concatenate([sph_ref[t, k : k + 1, :] for t in range(tiles)], 0) for k in range(3)]
-    moment = [
-        pos[1] * force[2] - pos[2] * force[1],
-        pos[2] * force[0] - pos[0] * force[2],
-        pos[0] * force[1] - pos[1] * force[0],
-    ]
+def wall_forces(slot_ref, order_ref, sums_ref, adds_ref):
+    lane = lax.broadcasted_iota(i32, (128, 128), 1) & 31
+    sums_ref[...] = jnp.zeros_like(sums_ref)
+
+    def four_tiles(i, carry):
+        for st in [4 * i + k for k in range(4)]:
+            last = [order_ref[2 + entry, st] for entry in range(2)]
+            highs, lows = [], []
+            for k in range(3):
+                value = slot_ref[0, last[0], k] + slot_ref[1, last[1], k]
+                high = value.astype(bf16)
+                highs.append(high)
+                lows.append((value - high.astype(f32)).astype(bf16))
+            added = jnp.dot(jnp.concatenate(highs + lows, 1), adds_ref[...], preferred_element_type=f32)
+            sums_ref[...] = jnp.where(lane == st, added, sums_ref[...])
+        return carry
+
+    lax.fori_loop(0, 4, four_tiles, 0)
+    turned = sums_ref[...].T
+    return [stiff_wall * turned[32 * k : 32 * k + 16] for k in range(3)]
+
+
+def wrench_line(entry, slot_ref, order_ref, wide_ref):
+    def one_tile(st, carry):
+        last = order_ref[2 + entry, st]
+        total = list(carry)
+        for group in range(16):
+            here = slice(8 * group, 8 * group + 8)
+            x, y, z = (slot_ref[entry, last, k, here, :] for k in range(3))
+            px, py, pz = (wide_ref[st, k, here, :] for k in range(3))
+            moment = (py * z - pz * y, pz * x - px * z, px * y - py * x)
+            total = [t + value for t, value in zip(total, (x, y, z, *moment))]
+        return tuple(total)
+
+    total = lax.fori_loop(0, 16, one_tile, (jnp.zeros((8, 128), f32),) * 6)
     lane = lax.broadcasted_iota(i32, (1, 128), 1)
     line = jnp.zeros((1, 128), f32)
-    for k, value in enumerate(force + moment):
-        line = jnp.where(lane == k, -jnp.sum(jnp.sum(value, 0, keepdims=True), 1, keepdims=True), line)
+    for k, value in enumerate(total):
+        value = jnp.sum(jnp.sum(value, 0, keepdims=True), 1, keepdims=True)
+        line = jnp.where(lane == k, -stiff_wall * value, line)
     return line
 
 
@@ -308,9 +342,9 @@
 
 def step_kernel(
     state_hbm, dest_hbm, body_hbm, code_hbm, tri_ref, state_out, kick_out,
-    state_ref, dest_ref, body_ref, code_ref, codes_ref,
+    state_ref, dest_ref, body_ref, code_ref,
     out1, got1, out2, sph, piece, sel_send, sel, names, names_got, names_smem,
-    wide, point, plain, linear, coef0, coef1, push0, push1, sums, adds, left, right, stacked, summed,
+    wide, point, plain, linear, coef0, coef1, slots, sums, adds, order, order_smem, left, right, stacked, summed,
     part, part_got, row, row_got,
     s1, r1, s2, r2, t1s, t1r, ns, nr, t2s, t2r, w1s, w1r, w2s, w2r, own_sem, names_sem,
     in0, in1, in2, in3, in4,
@@ -323,7 +357,6 @@
             (state_hbm, state_ref, in1),
             (body_hbm, body_ref, in2),
             (code_hbm, code_ref, in3),
-            (code_hbm, codes_ref, in4),
         )
     ]
     for copy in inputs:
@@ -335,6 +368,12 @@
     lane = lax.broadcasted_iota(i32, (1, 128), 1)
     names[...] = jnp.where(lane == 0, body_ref[0, 0], body_ref[0, 1])
     set_adds(adds)
+    for entry in range(2):
+        slots[entry, 32] = jnp.zeros((3, 128, 128), f32)
+    set_order(code_ref, order)
+    ordered = pltpu.make_async_copy(order, order_smem, in4)
+    ordered.start()
+    ordered.wait()
     pl.semaphore_wait(barrier, 2 * (N - 1))
 
     def along_sector(source, landing, sent, arrived):
@@ -425,18 +464,15 @@
     set_triangles(sel, plain, linear)
     body_row = lax.broadcasted_iota(i32, (N, 1, 128), 0)
     parts = jnp.zeros((N, 1, 128), f32)
-    wall = [jnp.zeros((16, 128), f32)] * 3
     for entry in range(2):
-        sums[entry] = jnp.zeros((128, 128), f32)
-        wall_tiles(code_ref, entry, plain, linear, wide, point, (coef0, coef1), (push0, push1), sums, adds)
-        force = wall_forces(codes_ref[entry : entry + 1, :], entry, sums)
-        wall = [w + g for w, g in zip(wall, force)]
-        parts = parts + jnp.where(body_row == body_ref[0, entry], wrench_line(sph, force)[None], 0.0)
+        wall_tiles(code_ref, entry, plain, linear, wide, point, (coef0, coef1), slots, order_smem)
+        parts = parts + jnp.where(body_row == body_ref[0, entry], wrench_line(entry, slots, order_smem, wide)[None], 0.0)
     part[...] = parts
 
     for peer in peers(sector):
         wrench_one(sector, peer).start()
     part_got[sector] = part[sector]
+    wall = wall_forces(slots, order_smem, sums, adds)
     pair_sums(PAIRS_ONE, PAIRS_TWO, left, right, stacked, summed)
     all_of(part_got, N - 1, w1r)
     row[...] = functools.reduce(jnp.add, [part_got[k] for k in range(N)])
@@ -467,7 +503,7 @@
         all_of(piece, HOLDERS, t1s)
 
 
-PAIRS_ONE, PAIRS_TWO, PAIRS_ALL = 3, 6, 8
+PAIRS_ONE, PAIRS_TWO, PAIRS_ALL = 3, 5, 8
 
 
 def step(state, dest, bodies, codes, tri):
@@ -486,7 +522,6 @@
             pltpu.VMEM(dest.shape, i32),
             pltpu.SMEM(bodies.shape, i32),
             pltpu.SMEM(codes.shape, i32),
-            pltpu.VMEM(codes.shape, i32),
             *[tiles] * 4,
             pltpu.VMEM((N, 3, 8, 128), f32),
             pltpu.VMEM((N, 2, 3, 8, 128), f32),
@@ -500,10 +535,11 @@
             pltpu.VMEM((2, 32, 8, 128), f32),
             pltpu.VMEM((128, 256), f32),
             pltpu.VMEM((128, 256), f32),
-            pltpu.VMEM((128, 768), bf16),
-            pltpu.VMEM((128, 768), bf16),
-            pltpu.VMEM((2, 128, 128), f32),
+            pltpu.VMEM((2, 33, 3, 128, 128), f32),
+            pltpu.VMEM((128, 128), f32),
             pltpu.VMEM((768, 128), bf16),
+            pltpu.VMEM((4, 128), i32),
+            pltpu.SMEM((4, 128), i32),
             pltpu.VMEM((slots, 32), bf16),
             pltpu.VMEM((32, slots), bf16),
             pltpu.VMEM((32, slots), bf16),

time: 53 us -> 47.8 us (0.902)
  Pallas kernels: 50.1 us -> 44.9 us
    pallas_call x1, Pallas kernels: 50.1 us -> 44.9 us  [step(): pl.pallas_call(step_kernel, out_shape=(jax.ShapeDtypeStruct((7, slots), f...]
where the time goes in v4:
time: 47.8 us; the launch traced here: 47.6 us
  Pallas kernels  44.9 us (94%)
  local copies, waits for them, and re-layouts  1.99 us (4%)
  between operations  0.65 us (1%)
    pallas_call x1, Pallas kernels, step(): pl.pallas_call(step_kernel, out_shape=(jax.ShapeDtypeStruct((7, slots), f...  44.9 us
    unnamed x4, local copies, waits for them, and re-layouts  1.99 us

profile of v4, /device:TPU:1, one launch (start us, length us, event | category | flops | bytes accessed | tf_op | source)
XLA Modules:
  0.0 47.6 jit_solution(12576454747175215472)
XLA Ops:
  0.6 44.9 %shard_map.68 = (f32[7,2048]{1,0:T(8,128)}, f32[1,6]{1,0:T(1,128)}) custom-call(f32[7,1024]{1,0:T(8,128)} %state_hbm.1, s32[1,1024]{1,0:T(1,128)} %bitcast.4, s32[1,2]{1,0:T(1,128)} %body_hbm.1, s32[2,32]{1,0:T(2,128)} %bitcast.5, f32[36,8,128]{2,1,0:T(8,128)} %bitcast.3), custom_call_target="tpu_custom_call" | custom-call | tf_op jit(solution)/shard_map/pallas_call | solution.py:515
  45.6 0.0 copy-start
  45.6 1.5 %copy.9 = f32[7,2048]{1,0:T(8,128)} copy(f32[7,2048]{1,0:T(8,128)} %get-tuple-element.4) | data formatting | bytes 114688
  47.0 0.0 copy-done
  47.1 0.5 %copy.10 = f32[1,6]{1,0:T(1,128)} copy(f32[1,6]{1,0:T(1,128)S(1)} %copy-done) | data formatting | bytes 48
Async XLA Ops:
  45.6 1.5 %copy-start = (f32[1,6]{1,0:T(1,128)S(1)}, f32[1,6]{1,0:T(1,128)}, u32[]{:S(2)}) copy-start(f32[1,6]{1,0:T(1,128)} %get-tuple-element.5) | copy-start | bytes 76

commit v5 on v4

--- a/solution.py
+++ b/solution.py
@@ -191,7 +191,6 @@
             c = jnp.maximum(c, 0.0)
             total = a + b + c
             inverse = pl.reciprocal(total, approx=True)
-            inverse = inverse * (2.0 - total * inverse)
             b, c = b * inverse, c * inverse
             ox = (wide_ref[st, 0, here, :] - ax) - b * ux - c * wx
             oy = (wide_ref[st, 1, here, :] - ay) - b * uy - c * wy
@@ -425,6 +424,8 @@
         own.start()
         names_got[sector] = names[...]
         own.wait()
+        all_of(names_got, N - 1, nr)
+        pltpu.make_async_copy(names_got, names_smem, names_sem).start()
 
     got1[bin_] = out1[bin_]
     all_of(got1, N - 1, r1)
@@ -436,11 +437,8 @@
 
     @pl.when(holding)
     def _():
-        all_of(names_got, N - 1, nr)
-        listed = pltpu.make_async_copy(names_got, names_smem, names_sem)
-        listed.start()
         all_of(piece, N - 1, t1r)
-        listed.wait()
+        pltpu.make_async_copy(names_got, names_smem, names_sem).wait()
         for dst in range(N):
             for entry in range(2):
                 sel_send[dst, entry] = piece[names_smem[dst, 0, entry]]
@@ -503,7 +501,7 @@
         all_of(piece, HOLDERS, t1s)
 
 
-PAIRS_ONE, PAIRS_TWO, PAIRS_ALL = 3, 5, 8
+PAIRS_ONE, PAIRS_TWO, PAIRS_ALL = 1, 4, 8
 
 
 def step(state, dest, bodies, codes, tri):
@@ -514,7 +512,7 @@
     tiles = pltpu.VMEM((N, 8, 128), f32)
     return pl.pallas_call(
         step_kernel,
-        out_shape=(jax.ShapeDtypeStruct((7, slots), f32), jax.ShapeDtypeStruct((1, 6), f32)),
+        out_shape=(pltpu.VMEM((7, slots), f32), pltpu.VMEM((1, 6), f32)),
         in_specs=[pl.BlockSpec(memory_space=pltpu.HBM)] * 5,
         out_specs=(vmem, vmem),
         scratch_shapes=[

time: 47.8 us -> 45 us (0.941)
  Pallas kernels: 44.9 us -> 43 us
  local copies, waits for them, and re-layouts: 1.99 us -> 1.14 us
    pallas_call x1, Pallas kernels: 44.9 us -> 43 us  [step(): pl.pallas_call(step_kernel, out_shape=(pltpu.VMEM((7, slots), f32), pltpu...]
    unnamed x4 -> x2, local copies, waits for them, and re-layouts: 1.99 us -> 1.14 us
where the time goes in v5:
time: 45 us; the launch traced here: 44.7 us
  Pallas kernels  43 us (96%)
  local copies, waits for them, and re-layouts  1.14 us (3%)
  between operations  0.64 us (1%)
    pallas_call x1, Pallas kernels, step(): pl.pallas_call(step_kernel, out_shape=(pltpu.VMEM((7, slots), f32), pltpu...  43 us
    unnamed x2, local copies, waits for them, and re-layouts  1.14 us

profile of v5, /device:TPU:1, one launch (start us, length us, event | category | flops | bytes accessed | tf_op | source)
XLA Modules:
  0.0 44.7 jit_solution(12435023891616422490)
XLA Ops:
  0.6 43.0 %shard_map.68 = (f32[7,2048]{1,0:T(8,128)S(1)}, f32[1,6]{1,0:T(1,128)S(1)}) custom-call(f32[7,1024]{1,0:T(8,128)} %state_hbm.1, s32[1,1024]{1,0:T(1,128)} %bitcast.4, s32[1,2]{1,0:T(1,128)} %body_hbm.1, s32[2,32]{1,0:T(2,128)} %bitcast.5, f32[36,8,128]{2,1,0:T(8,128)} %bitcast.3), custom_call_target="tpu_custom_call" | custom-call | tf_op jit(solution)/shard_map/pallas_call | solution.py:513
  43.6 0.6 %copy.9 = f32[7,2048]{1,0:T(8,128)} copy(f32[7,2048]{1,0:T(8,128)S(1)} %get-tuple-element.2) | data formatting | bytes 114688
  44.2 0.5 %copy.10 = f32[1,6]{1,0:T(1,128)} copy(f32[1,6]{1,0:T(1,128)S(1)} %get-tuple-element.3) | data formatting | bytes 48

commit v6 on v5

--- a/solution.py
+++ b/solution.py
@@ -158,16 +158,16 @@
             wide_ref[t, f] = jnp.broadcast_to(column, (128, 128))
 
 
-def wall_tiles(code_ref, entry, plain_ref, linear_ref, wide_ref, point_ref, coef_refs, slot_ref, order_ref):
+def wall_tiles(code_ref, plain_ref, linear_ref, wide_ref, point_ref, coef_refs, slot_refs, order_ref):
     count = code_ref.shape[1]
     upper = lax.broadcasted_iota(i32, (8, 128), 0) < 4
 
-    def tiles_of(n):
+    def tiles_of(entry, n):
         code = code_ref[entry, n]
         return code >> 5, code & 31
 
-    def weigh(n, coef_ref):
-        st, tt = tiles_of(n)
+    def weigh(entry, n, coef_ref):
+        st, tt = tiles_of(entry, n)
         high, middle, low = split3(linear_ref[entry, tt])
         rows = [high, middle, high, middle, low, high]
         for_b = jnp.concatenate([jnp.where(upper, g, 0.0) for g in rows], 0)
@@ -176,8 +176,9 @@
         points = point_ref[st]
         coef_ref[...] = jnp.dot(points, coefficients, preferred_element_type=f32)
 
-    def push(n, coef_ref):
-        st, tt = tiles_of(n)
+    def push(entry, n, coef_ref):
+        slot_ref = slot_refs[entry]
+        st, tt = tiles_of(entry, n)
         before = order_ref[entry, n]
         ax, ay, az, ux, uy, uz, wx, wy, wz = (
             jnp.broadcast_to(plain_ref[entry, tt, f : f + 1, :], (8, 128)) for f in range(9)
@@ -199,23 +200,28 @@
             return strength * ox, strength * oy, strength * oz
 
         def held(first):
-            return [[slot_ref[entry, before, k, 8 * g : 8 * g + 8, :] for k in range(3)] for g in range(first, first + 2)]
+            return [[slot_ref[before, k, 8 * g : 8 * g + 8, :] for k in range(3)] for g in range(first, first + 2)]
 
         for first in range(0, 16, 2):
             earlier = held(first)
             for g in range(2):
                 here = slice(8 * (first + g), 8 * (first + g) + 8)
                 for k, value in enumerate(eight(first + g)):
-                    slot_ref[entry, n, k, here, :] = earlier[g][k] + value
-
-    weigh(0, coef_refs[0])
+                    slot_ref[n, k, here, :] = earlier[g][k] + value
+
+    for entry in range(2):
+        weigh(entry, 0, coef_refs[entry])
 
     def two_tiles(i, carry):
         n = 2 * i
-        weigh(n + 1, coef_refs[1])
-        push(n, coef_refs[0])
-        weigh(jnp.minimum(n + 2, count - 1), coef_refs[0])
-        push(n + 1, coef_refs[1])
+        for entry in range(2):
+            weigh(entry, n + 1, coef_refs[2 + entry])
+        for entry in range(2):
+            push(entry, n, coef_refs[entry])
+        for entry in range(2):
+            weigh(entry, jnp.minimum(n + 2, count - 1), coef_refs[entry])
+        for entry in range(2):
+            push(entry, n + 1, coef_refs[2 + entry])
         return carry
 
     lax.fori_loop(0, count // 2, two_tiles, 0)
@@ -279,7 +285,7 @@
     lax.fori_loop(first, last, row_group, 0)
 
 
-def wall_forces(slot_ref, order_ref, sums_ref, adds_ref):
+def wall_forces(slot_refs, order_ref, sums_ref, adds_ref):
     lane = lax.broadcasted_iota(i32, (128, 128), 1) & 31
     sums_ref[...] = jnp.zeros_like(sums_ref)
 
@@ -288,7 +294,7 @@
             last = [order_ref[2 + entry, st] for entry in range(2)]
             highs, lows = [], []
             for k in range(3):
-                value = slot_ref[0, last[0], k] + slot_ref[1, last[1], k]
+                value = slot_refs[0][last[0], k] + slot_refs[1][last[1], k]
                 high = value.astype(bf16)
                 highs.append(high)
                 lows.append((value - high.astype(f32)).astype(bf16))
@@ -307,7 +313,7 @@
         total = list(carry)
         for group in range(16):
             here = slice(8 * group, 8 * group + 8)
-            x, y, z = (slot_ref[entry, last, k, here, :] for k in range(3))
+            x, y, z = (slot_ref[last, k, here, :] for k in range(3))
             px, py, pz = (wide_ref[st, k, here, :] for k in range(3))
             moment = (py * z - pz * y, pz * x - px * z, px * y - py * x)
             total = [t + value for t, value in zip(total, (x, y, z, *moment))]
@@ -343,7 +349,7 @@
     state_hbm, dest_hbm, body_hbm, code_hbm, tri_ref, state_out, kick_out,
     state_ref, dest_ref, body_ref, code_ref,
     out1, got1, out2, sph, piece, sel_send, sel, names, names_got, names_smem,
-    wide, point, plain, linear, coef0, coef1, slots, sums, adds, order, order_smem, left, right, stacked, summed,
+    wide, point, plain, linear, coef0, coef1, coef2, coef3, slots0, slots1, sums, adds, order, order_smem, left, right, stacked, summed,
     part, part_got, row, row_got,
     s1, r1, s2, r2, t1s, t1r, ns, nr, t2s, t2r, w1s, w1r, w2s, w2r, own_sem, names_sem,
     in0, in1, in2, in3, in4,
@@ -360,6 +366,7 @@
     ]
     for copy in inputs:
         copy.start()
+    slots = (slots0, slots1)
     barrier = greet(sector, bin_)
     for copy in inputs:
         copy.wait()
@@ -368,7 +375,7 @@
     names[...] = jnp.where(lane == 0, body_ref[0, 0], body_ref[0, 1])
     set_adds(adds)
     for entry in range(2):
-        slots[entry, 32] = jnp.zeros((3, 128, 128), f32)
+        slots[entry][32] = jnp.zeros((3, 128, 128), f32)
     set_order(code_ref, order)
     ordered = pltpu.make_async_copy(order, order_smem, in4)
     ordered.start()
@@ -462,9 +469,9 @@
     set_triangles(sel, plain, linear)
     body_row = lax.broadcasted_iota(i32, (N, 1, 128), 0)
     parts = jnp.zeros((N, 1, 128), f32)
+    wall_tiles(code_ref, plain, linear, wide, point, (coef0, coef1, coef2, coef3), slots, order_smem)
     for entry in range(2):
-        wall_tiles(code_ref, entry, plain, linear, wide, point, (coef0, coef1), slots, order_smem)
-        parts = parts + jnp.where(body_row == body_ref[0, entry], wrench_line(entry, slots, order_smem, wide)[None], 0.0)
+        parts = parts + jnp.where(body_row == body_ref[0, entry], wrench_line(entry, slots[entry], order_smem, wide)[None], 0.0)
     part[...] = parts
 
     for peer in peers(sector):
@@ -531,9 +538,9 @@
             pltpu.VMEM((N, 128, 48), bf16),
             pltpu.VMEM((2, 32, 16, 128), f32),
             pltpu.VMEM((2, 32, 8, 128), f32),
-            pltpu.VMEM((128, 256), f32),
-            pltpu.VMEM((128, 256), f32),
-            pltpu.VMEM((2, 33, 3, 128, 128), f32),
+            *[pltpu.VMEM((128, 256), f32)] * 4,
+            pltpu.VMEM((33, 3, 128, 128), f32),
+            pltpu.VMEM((33, 3, 128, 128), f32),
             pltpu.VMEM((128, 128), f32),
             pltpu.VMEM((768, 128), bf16),
             pltpu.VMEM((4, 128), i32),

time: 45 us -> 44.5 us (0.989)
  Pallas kernels: 43 us -> 42.5 us
where the time goes in v6:
time: 44.5 us; the launch traced here: 44.3 us
  Pallas kernels  42.5 us (96%)
  local copies, waits for them, and re-layouts  1.14 us (3%)
  between operations  0.64 us (1%)
    pallas_call x1, Pallas kernels, step(): pl.pallas_call(step_kernel, out_shape=(pltpu.VMEM((7, slots), f32), pltpu...  42.5 us
    unnamed x2, local copies, waits for them, and re-layouts  1.14 us

profile of v6, /device:TPU:1, one launch (start us, length us, event | category | flops | bytes accessed | tf_op | source)
XLA Modules:
  0.0 44.3 jit_solution(5090389955737056703)
XLA Ops:
  0.6 42.5 %shard_map.68 = (f32[7,2048]{1,0:T(8,128)S(1)}, f32[1,6]{1,0:T(1,128)S(1)}) custom-call(f32[7,1024]{1,0:T(8,128)} %state_hbm.1, s32[1,1024]{1,0:T(1,128)} %bitcast.4, s32[1,2]{1,0:T(1,128)} %body_hbm.1, s32[2,32]{1,0:T(2,128)} %bitcast.5, f32[36,8,128]{2,1,0:T(8,128)} %bitcast.3), custom_call_target="tpu_custom_call" | custom-call | tf_op jit(solution)/shard_map/pallas_call | solution.py:520
  43.2 0.6 %copy.9 = f32[7,2048]{1,0:T(8,128)} copy(f32[7,2048]{1,0:T(8,128)S(1)} %get-tuple-element.2) | data formatting | bytes 114688
  43.8 0.5 %copy.10 = f32[1,6]{1,0:T(1,128)} copy(f32[1,6]{1,0:T(1,128)S(1)} %get-tuple-element.3) | data formatting | bytes 48
